TPU v7x, 256 devices: a whole 4x4x8 slice. The times are simulated.
256 devices in a mesh: dp: 16 (over z, core), mp: 16 (over x, y).
Axes of the slice: x: 4, y: 4, z: 8, core: 2. Of those that a mesh axis runs over, the one named last changes fastest.
Arguments:
- tokens: bfloat16 [163840, 8192], P(('dp', 'mp')), may hold values from -24 to 24
- out_grads: bfloat16 [163840, 2, 128], P(('dp', 'mp')), may hold values from -0.0625 to 0.0625
- momentum: float32 [16, 8192, 2, 128], P('dp', 'mp'), may hold values from -6 to 6
- selected: int32 [128, 2, 2, 32], P('mp'), may hold values from 0 to 4095, as said below
Outputs:
- new_momentum: float32 [16, 8192, 2, 128], P('dp', 'mp')
- update: float32 [8192, 2, 128], P('mp')
Inputs may be any that keep to these rules, and one draw needn't show every extreme that they name: `selected`: within each span the 32 indices are distinct.
All inputs are finite; a program needn't handle non-finite values.
Results may differ from a plain program's by a relative error of at most 0.0003.
Values sent between devices are 32-bit elements; how exact they have to be, the bound alone decides.
No kernel may reach another device: no remote copies, remote signals or barrier semaphores. Data moves between devices by JAX's collectives and lax.ppermute only.
A program may use at most 128 MiB of HBM per device.

v0:
```python
import math

import jax
import jax.numpy as jnp
from jax import lax
from jax.sharding import PartitionSpec as P

SPAN = 64


momentum_decay = 0.9
highest = lax.Precision.HIGHEST


def dct_basis(length):
    frequency = jnp.arange(length, dtype=jnp.float32)[:, None]
    position = jnp.arange(length, dtype=jnp.float32)[None, :]
    basis = jnp.cos(math.pi * (2.0 * position + 1.0) * frequency / (2.0 * length)) * math.sqrt(
        2.0 / length
    )
    scaling = jnp.where(frequency == 0.0, math.sqrt(0.5), 1.0)
    return basis * scaling


def forward_spans(values, basis):
    rows, mats, cols = values.shape
    blocks = values.reshape(rows // SPAN, SPAN, mats, cols // SPAN, SPAN)
    coeffs = jnp.einsum("ua,ramck,vk->rmcuv", basis, blocks, basis, precision=highest)
    return coeffs.reshape(rows // SPAN, mats, cols // SPAN, SPAN * SPAN)


def inverse_spans(coeffs, basis):
    crows, mats, ccols, _ = coeffs.shape
    square = coeffs.reshape(crows, mats, ccols, SPAN, SPAN)
    blocks = jnp.einsum("ua,rmcuv,vk->ramck", basis, square, basis, precision=highest)
    return blocks.reshape(crows * SPAN, mats, ccols * SPAN)


def spread_values(values, matches):
    return jnp.sum(jnp.where(matches, values[..., None], 0.0), axis=-2)


def normalize(decoded):
    rows, mats, cols = decoded.shape
    view = decoded.reshape(rows // SPAN, SPAN, mats, cols // SPAN, SPAN)
    power = jnp.mean(view * view, axis=(1, 4), keepdims=True)
    return (view / jnp.sqrt(power + 1e-06)).reshape(decoded.shape)


def on_device(tokens, out_grads, momentum, selected):
    rows_local = momentum.shape[1]
    mat_count = momentum.shape[2]
    col_count = momentum.shape[3]
    flat_grads = out_grads.reshape(out_grads.shape[0], mat_count * col_count)
    full_sum = lax.psum(
        lax.dot_general(
            tokens, flat_grads, (((0,), (0,)), ((), ())), preferred_element_type=jnp.float32
        ),
        "mp",
    )
    gradient = lax.dynamic_slice_in_dim(full_sum, lax.axis_index("mp") * rows_local, rows_local, 0)
    basis = dct_basis(SPAN)
    blend = momentum_decay * momentum[0] + gradient.reshape(rows_local, mat_count, col_count)
    coeffs = forward_spans(blend, basis)
    chosen = jnp.take_along_axis(coeffs, selected, axis=3)
    positions = jnp.arange(SPAN * SPAN, dtype=jnp.int32)
    matches = selected[..., None] == positions
    new_momentum = blend - inverse_spans(spread_values(chosen, matches), basis)
    packed = chosen.reshape(1, chosen.size)
    gathered = lax.all_gather(packed, "dp", axis=0, tiled=True)
    summed = jnp.sum(gathered, axis=0)
    summed = summed.reshape(chosen.shape)
    decoded = inverse_spans(spread_values(summed, matches), basis)
    return (new_momentum[None], normalize(decoded))


def solution(mesh):
    return jax.shard_map(
        on_device,
        mesh=mesh,
        in_specs=(
            P(("dp", "mp"), None),
            P(("dp", "mp"), None, None),
            P("dp", "mp", None, None),
            P("mp", None, None, None),
        ),
        out_specs=(P("dp", "mp", None, None), P("mp", None, None)),
        check_vma=False,
    )
```

profile of v0, /device:TPU:8, one launch (start us, length us, event | category | flops | bytes accessed | tf_op | source)
XLA Modules:
  0.0 231.5 jit_solution(7541063787900167464)
XLA Ops:
  7.2 0.0 all-reduce.2.cloned.1.call-start
  7.2 0.0 copy-start
  7.2 10.7 %fusion.2 = f32[8192,256]{1,0:T(8,128)} fusion(bf16[640,8192]{1,0:T(8,128)(2,1)} %param.4, bf16[80,8,2,128]{3,2,1,0:T(2,128)(2,1)} %bitcast.49), kind=kOutput, calls=%fused_computation.10 | convolution fusion | flops 2684354560 | bytes 19202048 | tf_op jit(solution)/shard_map/dot_general | solution.py:56
  18.0 0.0 copy-start.1
  18.0 0.0 all-reduce.2.cloned.1.call-update
  18.0 0.0 copy-done
  18.0 0.2 copy.48
  18.2 0.1 broadcast_multiply_fusion
  18.3 0.2 mul.150
  18.5 0.2 copy-done.1
  18.7 0.1 reshape.101
  18.8 152.6 %all-reduce.2.cloned.1.call-done = f32[8192,256]{1,0:T(8,128)} async-done(((f32[8192,256]{1,0:T(8,128)}), f32[8192,256]{1,0:T(8,128)}) %all-reduce.2.cloned.1.call-update) | async-done | bytes 8388624 | tf_op jit(solution)/shard_map/psum | solution.py:55
  171.4 1.1 constant_dynamic-slice_fusion
  172.5 0.2 copy.49
  172.7 0.2 reshape.94
  172.9 0.1 add.56
  173.0 3.2 %fusion = f32[8,2,2,64,64]{3,4,2,1,0:T(8,128)S(1)} fusion(f32[8,64,2,2,64]{1,0,4,3,2:T(8,128)S(1)} %add.56, f32[64]{0:T(128)S(1)} %get-tuple-element.16, f32[64]{0:T(128)S(1)} %get-tuple-element.17), kind=kOutput, calls=%fused_computation.5 | convolution fusion | flops 100675584 | bytes 1049088 | tf_op jit(solution)/shard_map/ua,ramck,vk->rmcuv/dot_general | solution.py:28
  176.2 1.1 fusion.12
  177.3 0.5 reshape.95
  177.9 11.6 %gather_fusion = f32[1024]{0:T(1024)S(1)} fusion(f32[8,2,2,4096]{3,2,1,0:T(2,128)S(1)} %reshape.95, s32[1024]{0:T(1024)S(1)} %reshape.101), kind=kCustom, calls=%fused_computation | custom fusion | bytes 24576 | tf_op jit(solution)/shard_map/jit(take_along_axis)/gather | solution.py:65
  189.5 0.1 reshape.104
  189.6 0.1 reshape.112
  189.7 17.8 %all-gather = f32[16,1,1024]{2,1,0:T(1,128)S(1)} all-gather(f32[1,1,1024]{2,1,0:T(1,128)S(1)} %reshape.112), channel_id=1, replica_groups=mesh['dp'=16,'mp'=16] {'dp'}, dimensions={0}, use_global_device_ids=true | all-gather | bytes 69632 | tf_op jit(solution)/shard_map/all_gather | solution.py:70
  207.4 0.1 reduce_sum.37
  207.5 0.1 broadcast_in_dim.41
  207.6 6.7 %select_reduce_fusion = (f32[8,2,2,4096]{3,2,1,0:T(2,128)S(1)}, f32[8,2,2,4096]{3,2,1,0:T(2,128)S(1)}) fusion(f32[8,2,2,32]{3,2,1,0:T(2,128)S(1)} %broadcast_in_dim.41, s32[8,2,2,32]{3,2,1,0:T(2,128)S(1)} %copy-done.1, f32[8,2,2,32]{3,2,1,0:T(2,128)S(1)} %and_select_fusion), kind=kLoop, calls=%fused_computation.1 | loop fusion | flops 20709376 | bytes 1060864 | tf_op jit(solution)/shard_map/reduce_sum | solution.py:40
  214.2 0.6 reshape.117
  214.9 1.2 fusion.7
  216.0 1.2 multiply_reduce_fusion
  217.3 0.1 divide_bitcast_fusion
  217.4 0.8 copy.73
  218.2 1.7 reshape.118
  220.0 0.6 reshape.116
  220.6 1.2 fusion.10
  221.7 1.1 convolution_bitcast_fusion
  222.8 0.4 copy.56
  223.2 0.3 reshape.98
  223.5 0.2 add_subtract_fusion
  223.7 1.0 copy.61
  (4 shorter events, 0.1 us)
Async XLA Ops:
  7.2 164.3 %all-reduce.2.cloned.1.call-start = ((), (), s32[]{:S(2)}) async-start(), calls=%async_computation | async-start | bytes 16777216 | tf_op jit(solution)/shard_map/psum | solution.py:55
  7.2 10.8 %copy-start = (f32[1,512,2,128]{3,2,1,0:T(2,128)S(1)}, f32[1,512,2,128]{3,2,1,0:T(2,128)}, u32[]{:S(2)}) copy-start(f32[1,512,2,128]{3,2,1,0:T(2,128)} %param.6) | copy-start | bytes 1572868
  18.0 0.7 copy-start.1
Sparse Core Ops, SparseCore 0:
  18.1 153.2 all-reduce.1
where the time goes:
time: 234 us; the launch traced here: 232 us
  waiting for transfers between devices  153 us (65%)
  local copies, waits for them, and re-layouts  20 us (9%)
  matrix products  19.6 us (8%)
  blocking collectives  17.8 us (8%)
  between operations  14.2 us (6%)
  other arithmetic  7.25 us (3%)
    psum x1, waiting for transfers between devices, on_device(): lax.psum(lax.dot_general(tokens, flat_grads, (((0,), (0,)), ((), ())), pr...  153 us
    all_gather x1, blocking collectives, on_device(): gathered = lax.all_gather(packed, 'dp', axis=0, tiled=True)  17.8 us
    gather x3, local copies, waits for them, and re-layouts, on_device(): chosen = jnp.take_along_axis(coeffs, selected, axis=3)  11.7 us
    dot_general x1, matrix products, on_device(): lax.dot_general(tokens, flat_grads, (((0,), (0,)), ((), ())), preferred_e...  10.7 us
    reduce_sum x1, other arithmetic, spread_values(): return jnp.sum(jnp.where(matches, values[..., None], 0.0), axis=-2)  6.67 us
  transfers between devices with their start and end apart: 1, of which 1 were waited for; matrix products, arithmetic and copies ran while one was open for 0% of the time, Pallas kernels for 0%

commit v1 on v0

v1 whole, which is shorter than its diff:
```python
import functools
import math

import jax
import jax.numpy as jnp
import numpy as np
from jax import lax
from jax.experimental import pallas as pl
from jax.experimental.pallas import tpu as pltpu
from jax.sharding import PartitionSpec as P

SPAN = 64
SIDE = 4
DECAY = 0.9
HIGHEST = lax.Precision.HIGHEST


def dct_basis(n):
    u = np.arange(n)[:, None].astype(np.float64)
    a = np.arange(n)[None, :].astype(np.float64)
    basis = np.cos(math.pi * (2.0 * a + 1.0) * u / (2.0 * n)) * math.sqrt(2.0 / n)
    basis[0] *= math.sqrt(0.5)
    return basis.astype(np.float32)


def shift_pairs(n_dp, primary, step):
    pairs = []
    n_mp = SIDE * SIDE
    for dp in range(n_dp):
        for x in range(SIDE):
            for y in range(SIDE):
                along_x = (dp % 2 == 0) == primary
                to = ((x + step) % SIDE, y) if along_x else (x, (y + step) % SIDE)
                pairs.append((dp * n_mp + x * SIDE + y, dp * n_mp + to[0] * SIDE + to[1]))
    return pairs


def matmul_kernel(table, grads_t, tokens, low, high):
    half = low.shape[-1]
    g = grads_t[...]
    low[0] = jnp.dot(g, tokens[:, :half], preferred_element_type=jnp.float32)
    high[0] = jnp.dot(g, tokens[:, half:], preferred_element_type=jnp.float32)


def partial_halves(table, grads_t, tokens, rows):
    cols, toks = grads_t.shape
    count = table.shape[0]
    half = rows // 2
    out = jax.ShapeDtypeStruct((count, cols, half), jnp.float32)
    out_spec = pl.BlockSpec((1, cols, half), lambda i, t: (i, 0, 0))
    return pl.pallas_call(
        matmul_kernel,
        grid_spec=pltpu.PrefetchScalarGridSpec(
            num_scalar_prefetch=1,
            grid=(count,),
            in_specs=[
                pl.BlockSpec((cols, toks), lambda i, t: (0, 0)),
                pl.BlockSpec((toks, rows), lambda i, t: (0, t[i])),
            ],
            out_specs=[out_spec, out_spec],
        ),
        out_shape=[out, out],
        compiler_params=pltpu.CompilerParams(vmem_limit_bytes=32 * 1024 * 1024),
        cost_estimate=pl.CostEstimate(
            flops=2 * count * rows * cols * toks,
            bytes_accessed=count * rows * (2 * toks + 4 * cols),
            transcendentals=0,
        ),
    )(table, grads_t, tokens)


def chosen_kernel(blend, left, right, chosen):
    spans = left.shape[0]
    for i in range(spans):
        x = blend[:, i * SPAN : (i + 1) * SPAN]
        w = jnp.dot(left[i], x, precision=HIGHEST, preferred_element_type=jnp.float32)
        chosen[i] = jnp.sum(w * right[i], axis=1, keepdims=True)


def decode(values, left, right, i):
    return lax.dot_general(
        left[i],
        values * right[i],
        (((0,), (0,)), ((), ())),
        precision=HIGHEST,
        preferred_element_type=jnp.float32,
    )


def momentum_kernel(blend, chosen, left, right, out):
    mats, lanes = out.shape[1], out.shape[2]
    for i in range(left.shape[0]):
        rows = slice(i * SPAN, (i + 1) * SPAN)
        new = blend[:, rows] - decode(chosen[i], left, right, i)
        for m in range(mats):
            out[rows, m, :] = new[m * lanes : (m + 1) * lanes].T


def update_kernel(gathered, left, right, out):
    mats, lanes = out.shape[1], out.shape[2]
    for i in range(left.shape[0]):
        rows = slice(i * SPAN, (i + 1) * SPAN)
        summed = jnp.sum(gathered[:, i], axis=0)
        decoded = decode(summed, left, right, i)
        cols = decoded.shape[0]
        square = (decoded * decoded).reshape(cols // SPAN, SPAN, SPAN)
        power = jnp.sum(jnp.sum(square, axis=1, keepdims=True), axis=2, keepdims=True) / (SPAN * SPAN)
        scaled = (decoded.reshape(square.shape) / jnp.sqrt(power + 1e-06)).reshape(decoded.shape)
        for m in range(mats):
            out[rows, m, :] = scaled[m * lanes : (m + 1) * lanes].T


def on_device(n_dp, tokens, out_grads, momentum, selected):
    rows, mats, lanes = momentum.shape[1:]
    cols = mats * lanes
    spans = rows // SPAN
    ccols = lanes // SPAN
    kept = selected.shape[-1]
    core = lax.axis_index("dp") % 2
    mp = lax.axis_index("mp")
    x, y = mp // SIDE, mp % SIDE
    p = jnp.where(core == 0, x, y)
    s = jnp.where(core == 0, y, x)
    away = jnp.arange(SIDE, dtype=jnp.int32)

    def blocks(dp_):
        to_p, to_s = (p + dp_) % SIDE, (s + away) % SIDE
        return jnp.where(core == 0, to_p * SIDE + to_s, to_s * SIDE + to_p).astype(jnp.int32)

    def send(v, primary, step):
        return lax.ppermute(v, ("dp", "mp"), shift_pairs(n_dp, primary, step))

    grads_t = out_grads.reshape(out_grads.shape[0], cols).T
    a_lo, a_hi = partial_halves(blocks(2), grads_t, tokens, rows)
    ra_lo = send(a_lo, True, -1)
    ra_hi = send(a_hi, True, 1)
    back_lo, back_hi = partial_halves(blocks(3), grads_t, tokens, rows)
    rb_hi = send(back_hi, True, -1)
    fore_lo, fore_hi = partial_halves(blocks(1), grads_t, tokens, rows)
    rb_lo = send(fore_lo, True, 1)
    own_lo, own_hi = partial_halves(blocks(0), grads_t, tokens, rows)
    rc_lo = send(back_lo + ra_lo, True, -1)
    rc_hi = send(fore_hi + ra_hi, True, 1)
    s_lo = [own_lo[k] + rc_lo[k] + rb_lo[k] for k in range(SIDE)]
    s_hi = [own_hi[k] + rb_hi[k] + rc_hi[k] for k in range(SIDE)]
    ta_lo = send(s_lo[2], False, -1)
    ta_hi = send(s_hi[2], False, 1)
    tb_hi = send(s_hi[3], False, -1)
    tb_lo = send(s_lo[1], False, 1)
    tc_lo = send(s_lo[3] + ta_lo, False, -1)
    tc_hi = send(s_hi[1] + ta_hi, False, 1)

    basis = jnp.asarray(dct_basis(SPAN))
    flat = selected.reshape(spans, mats * ccols * kept)
    places = jnp.arange(SPAN, dtype=jnp.int32)

    def basis_rows(index):
        hot = (index[..., None] == places).astype(jnp.float32)
        return jnp.einsum("ikp,pa->ika", hot, basis, precision=HIGHEST)

    right = basis_rows(flat // SPAN)
    narrow = basis_rows(flat % SPAN)
    group = jnp.arange(mats * ccols * kept) // kept
    column = jnp.arange(cols) // SPAN
    left = jnp.where(group[:, None] == column[None, :], jnp.tile(narrow, (1, 1, mats * ccols)), 0.0)

    faded_t = DECAY * momentum[0].reshape(rows, cols).T
    blend = faded_t + jnp.concatenate([s_lo[0] + tc_lo + tb_lo, s_hi[0] + tb_hi + tc_hi], axis=1)
    chosen = pl.pallas_call(
        chosen_kernel,
        out_shape=jax.ShapeDtypeStruct((spans, mats * ccols * kept, 1), jnp.float32),
    )(blend, left, right)
    packed = chosen.reshape(1, spans, mats * ccols * kept)
    gathered = lax.all_gather(packed, "dp", axis=0, tiled=True)[..., None]
    out_shape = jax.ShapeDtypeStruct((rows, mats, lanes), jnp.float32)
    new_momentum = pl.pallas_call(momentum_kernel, out_shape=out_shape)(blend, chosen, left, right)
    update = pl.pallas_call(update_kernel, out_shape=out_shape)(gathered, left, right)
    return new_momentum[None], update


def solution(mesh):
    return jax.shard_map(
        functools.partial(on_device, mesh.shape["dp"]),
        mesh=mesh,
        in_specs=(
            P(("dp", "mp"), None),
            P(("dp", "mp"), None, None),
            P("dp", "mp", None, None),
            P("mp", None, None, None),
        ),
        out_specs=(P("dp", "mp", None, None), P("mp", None, None)),
        check_vma=False,
    )
```

time: 234 us -> 119 us (0.51)
  the two profiles are of different devices: /device:TPU:8 before, /device:TPU:7 now
where the time goes in v1:
time: 119 us; the launch traced here: 118 us
  blocking collectives  28 us (24%)
  Pallas kernels  26 us (22%)
  local copies, waits for them, and re-layouts  21.1 us (18%)
  other arithmetic  15.2 us (13%)
  starting transfers between devices  13.9 us (12%)
  waiting for transfers between devices  11.6 us (10%)
  matrix products  1.5 us (1%)
    all_gather x1, blocking collectives, on_device(): gathered = lax.all_gather(packed, 'dp', axis=0, tiled=True)[..., None]  28 us
    ppermute x12, starting transfers between devices, send(): return lax.ppermute(v, ('dp', 'mp'), shift_pairs(n_dp, primary, step))  13.9 us
    unnamed x19, local copies, waits for them, and re-layouts  13.3 us
    ppermute x12, waiting for transfers between devices, send(): return lax.ppermute(v, ('dp', 'mp'), shift_pairs(n_dp, primary, step))  11.6 us
    pallas_call x4, Pallas kernels, partial_halves(): pl.pallas_call(matmul_kernel, grid_spec=pltpu.PrefetchScalarGridSpec(num_...  11.3 us
    pallas_call x1, Pallas kernels, on_device(): pl.pallas_call(update_kernel, out_shape=out_shape)(gathered, left, right)  6.37 us
    pallas_call x1, Pallas kernels, on_device(): pl.pallas_call(momentum_kernel, out_shape=out_shape)  4.94 us
    broadcast_in_dim x1, local copies, waits for them, and re-layouts, on_device(): gathered = lax.all_gather(packed, 'dp', axis=0, tiled=True)[..., None]  4.68 us
  transfers between devices with their start and end apart: 12, of which 6 were waited for; matrix products, arithmetic and copies ran while one was open for 14% of the time, Pallas kernels for 7%

profile of v1, /device:TPU:7, one launch (start us, length us, event | category | flops | bytes accessed | tf_op | source)
XLA Modules:
  0.0 118.2 jit_solution(8828757548637750071)
XLA Ops:
  0.7 1.3 %copy.27 = bf16[640,2,128]{0,2,1:T(8,128)(2,1)S(1)} copy(bf16[640,2,128]{2,1,0:T(2,128)(2,1)} %param.6) | data formatting | bytes 655360 | tf_op args[1]
  2.1 0.0 copy-start
  2.1 4.0 %copy-done = bf16[640,8192]{1,0:T(8,128)(2,1)S(1)} copy-done((bf16[640,8192]{1,0:T(8,128)(2,1)S(1)}, bf16[640,8192]{1,0:T(8,128)(2,1)}, u32[]{:S(2)}) %copy-start) | copy-done | bytes 10485784
  6.1 3.5 %shard_map.70 = (f32[4,256,256]{2,1,0:T(8,128)}, f32[4,256,256]{2,1,0:T(8,128)}) custom-call(s32[4]{0:T(128)S(1)} %get-tuple-element.25.table, bf16[256,640]{1,0:T(8,128)(2,1)S(1)} %bitcast.41, bf16[640,8192]{1,0:T(8,128)(2,1)S(1)} %copy-done), custom_call_target="tpu_custom_call" | custom-call | flops 671088640 | bytes 4718592 | tf_op jit(solution)/shard_map/pallas_call | solution.py:51
  9.6 2.7 %collective-permute-start = (f32[4,256,256]{2,1,0:T(8,128)}, f32[4,256,256]{2,1,0:T(8,128)}, u32[]{:S(2)}, u32[]{:S(2)}) collective-permute-start(f32[4,256,256]{2,1,0:T(8,128)} %get-tuple-element.12), channel_id=1, source_target_pairs={{0,12},{1,13},{2,14},{3,15},{4,0},{5,1},{6,2},{7,3},{8,4},{9,5},{1... | collective-permute-start | bytes 3145736 | tf_op jit(solution)/shard_map/ppermute | solution.py:131
  12.3 0.0 collective-permute-start.7
  12.3 0.0 copy-done.1
  12.3 2.3 %shard_map.71 = (f32[4,256,256]{2,1,0:T(8,128)S(1)}, f32[4,256,256]{2,1,0:T(8,128)S(1)}) custom-call(s32[4]{0:T(128)S(1)} %get-tuple-element.24.table, bf16[256,640]{1,0:T(8,128)(2,1)S(1)} %bitcast.42, bf16[640,8192]{1,0:T(8,128)(2,1)S(1)} %copy-done.1), custom_call_target="tpu_custom_call" | custom-call | flops 671088640 | bytes 4718592 | tf_op jit(solution)/shard_map/pallas_call | solution.py:51
  14.6 0.1 collective-permute-start.2
  14.7 0.0 copy-start.2
  14.8 4.0 %copy-done.2 = bf16[640,8192]{1,0:T(8,128)(2,1)S(1)} copy-done((bf16[640,8192]{1,0:T(8,128)(2,1)S(1)}, bf16[640,8192]{1,0:T(8,128)(2,1)}, u32[]{:S(2)}) %copy-start.2) | copy-done | bytes 10485784
  18.8 3.3 %shard_map.69 = (f32[4,256,256]{2,1,0:T(8,128)S(1)}, f32[4,256,256]{2,1,0:T(8,128)}) custom-call(s32[4]{0:T(128)S(1)} %get-tuple-element.26.table, bf16[256,640]{1,0:T(8,128)(2,1)S(1)} %bitcast.43, bf16[640,8192]{1,0:T(8,128)(2,1)S(1)} %copy-done.2), custom_call_target="tpu_custom_call" | custom-call | flops 671088640 | bytes 4718592 | tf_op jit(solution)/shard_map/pallas_call | solution.py:51
  22.0 2.7 %collective-permute-start.6 = (f32[4,256,256]{2,1,0:T(8,128)}, f32[4,256,256]{2,1,0:T(8,128)}, u32[]{:S(2)}, u32[]{:S(2)}) collective-permute-start(f32[4,256,256]{2,1,0:T(8,128)} %get-tuple-element.15), channel_id=1, source_target_pairs={{0,12},{1,13},{2,14},{3,15},{4,0},{5,1},{6,2},{7,3},{8,4},{9,5},{1... | collective-permute-start | bytes 3145736 | tf_op jit(solution)/shard_map/ppermute | solution.py:131
  24.7 0.0 copy-done.8
  24.7 0.1 reshape.111
  24.8 0.0 collective-permute-done
  24.8 2.3 %add.255 = f32[4,256,256]{2,1,0:T(8,128)} add(f32[4,256,256]{2,1,0:T(8,128)S(1)} %get-tuple-element.11, f32[4,256,256]{2,1,0:T(8,128)} %collective-permute-done) | non-fusion elementwise | flops 262144 | bytes 3145728 | tf_op jit(solution)/shard_map/add | solution.py:142
  27.1 3.0 %collective-permute-start.1 = (f32[4,256,256]{2,1,0:T(8,128)}, f32[4,256,256]{2,1,0:T(8,128)}, u32[]{:S(2)}, u32[]{:S(2)}) collective-permute-start(f32[4,256,256]{2,1,0:T(8,128)} %add.255), channel_id=1, source_target_pairs={{0,12},{1,13},{2,14},{3,15},{4,0},{5,1},{6,2},{7,3},{8,4},{9,5},{1... | collective-permute-start | bytes 3145736 | tf_op jit(solution)/shard_map/ppermute | solution.py:131
  30.1 0.0 copy-done.7
  30.1 0.3 fusion.14
  30.4 0.1 tile.4
  30.5 1.4 %copy.28 = f32[8,128,256]{2,1,0:T(8,128)} copy(f32[8,128,256]{1,2,0:T(8,128)S(1)} %bitcast.45) | data formatting | bytes 2097152 | tf_op jit(solution)/shard_map/tile | solution.py:165
  31.9 0.0 collective-permute-done.7
  31.9 1.5 %add.278 = f32[4,256,256]{2,1,0:T(8,128)S(1)} add(f32[4,256,256]{2,1,0:T(8,128)S(1)} %get-tuple-element.16, f32[4,256,256]{2,1,0:T(8,128)} %collective-permute-done.7) | non-fusion elementwise | flops 262144 | bytes 3145728 | tf_op jit(solution)/shard_map/add | solution.py:143
  33.4 0.1 collective-permute-start.8
  33.5 0.0 copy-start.3
  33.5 4.0 %copy-done.3 = bf16[640,8192]{1,0:T(8,128)(2,1)S(1)} copy-done((bf16[640,8192]{1,0:T(8,128)(2,1)S(1)}, bf16[640,8192]{1,0:T(8,128)(2,1)}, u32[]{:S(2)}) %copy-start.3) | copy-done | bytes 10485784
  37.5 2.3 %shard_map.68 = (f32[4,256,256]{2,1,0:T(8,128)S(1)}, f32[4,256,256]{2,1,0:T(8,128)S(1)}) custom-call(s32[4]{0:T(128)S(1)} %get-tuple-element.27.table, bf16[256,640]{1,0:T(8,128)(2,1)S(1)} %bitcast.44, bf16[640,8192]{1,0:T(8,128)(2,1)S(1)} %copy-done.3), custom_call_target="tpu_custom_call" | custom-call | flops 671088640 | bytes 4718592 | tf_op jit(solution)/shard_map/pallas_call | solution.py:51
  39.8 0.1 broadcast_compare_fusion
  39.9 0.0 copy-done.4
  39.9 1.2 broadcast_select_fusion.left
  41.1 0.0 collective-permute-done.2
  41.1 6.9 %collective-permute-done.1 = f32[4,256,256]{2,1,0:T(8,128)} collective-permute-done((f32[4,256,256]{2,1,0:T(8,128)}, f32[4,256,256]{2,1,0:T(8,128)}, u32[]{:S(2)}, u32[]{:S(2)}) %collective-permute-start.1) | collective-permute-done | bytes 1048608 | tf_op jit(solution)/shard_map/ppermute | solution.py:131
  48.0 2.0 %fusion.8 = (f32[256,256]{1,0:T(8,128)S(1)}, f32[256,256]{1,0:T(8,128)}) fusion(f32[4,256,256]{2,1,0:T(8,128)} %collective-permute-done.2, f32[4,256,256]{2,1,0:T(8,128)} %collective-permute-done.1, f32[4,256,256]{2,1,0:T(8,128)S(1)} %get-tuple-element.10), kind=kLoop, calls=%fused_computation.21 | loop fusion | flops 262144 | bytes 2097152 | tf_op jit(solution)/shard_map/add | solution.py:144
  50.0 0.6 collective-permute-start.3
  50.5 0.0 copy-done.6
  50.5 0.3 broadcast_multiply_fusion
  50.8 2.2 %collective-permute-start.5 = (f32[256,256]{1,0:T(8,128)}, f32[256,256]{1,0:T(8,128)}, u32[]{:S(2)}, u32[]{:S(2)}) collective-permute-start(f32[256,256]{1,0:T(8,128)} %get-tuple-element.19), channel_id=1, source_target_pairs={{0,1},{1,2},{2,3},{3,0},{4,5},{5,6},{6,7},{7,4},{8,9},{9,10},{10,1... | collective-permute-start | bytes 786440 | tf_op jit(solution)/shard_map/ppermute | solution.py:131
  53.0 0.0 collective-permute-done.6
  53.0 0.0 collective-permute-done.8
  53.0 2.3 %fusion.3 = (f32[256,256]{1,0:T(8,128)}, f32[256,256]{1,0:T(8,128)}) fusion(f32[4,256,256]{2,1,0:T(8,128)S(1)} %collective-permute-done.8, f32[4,256,256]{2,1,0:T(8,128)} %collective-permute-done.6, f32[4,256,256]{2,1,0:T(8,128)S(1)} %get-tuple-element.14), kind=kLoop, calls=%fused_computation.10 | loop fusion | flops 262144 | bytes 2097152 | tf_op jit(solution)/shard_map/add | solution.py:145
  55.3 0.0 collective-permute-start.10
  55.3 1.1 collective-permute-done.3
  56.4 1.1 fusion.10
  57.5 0.5 collective-permute-start.4
  58.0 1.2 %fusion.16.right = f32[8,128,64]{2,1,0:T(8,128)} fusion(f32[64,64,1]{0,1,2:T(8,128)S(1)} %copy-done.7, s32[8,128]{1,0:T(8,128)S(1)} %get-tuple-element.22), kind=kOutput, calls=%fused_computation.37 | convolution fusion | flops 50462720 | bytes 282624 | tf_op jit(solution)/shard_map/ikp,pa->ika/dot_general | solution.py:159
  59.2 0.2 copy.26
  59.4 0.3 collective-permute-start.9
  59.7 1.5 %collective-permute-done.10 = f32[256,256]{1,0:T(8,128)} collective-permute-done((f32[256,256]{1,0:T(8,128)}, f32[256,256]{1,0:T(8,128)}, u32[]{:S(2)}, u32[]{:S(2)}) %collective-permute-start.10) | collective-permute-done | bytes 262176 | tf_op jit(solution)/shard_map/ppermute | solution.py:131
  61.1 1.2 fusion.2
  62.3 1.8 %collective-permute-start.11 = (f32[256,256]{1,0:T(8,128)S(1)}, f32[256,256]{1,0:T(8,128)S(1)}, u32[]{:S(2)}, u32[]{:S(2)}) collective-permute-start(f32[256,256]{1,0:T(8,128)S(1)} %fusion.2), channel_id=1, source_target_pairs={{0,1},{1,2},{2,3},{3,0},{4,5},{5,6},{6,7},{7,4},{8,9},{9,10},{10,1... | collective-permute-start | bytes 786440 | tf_op jit(solution)/shard_map/ppermute | solution.py:131
  64.1 0.0 collective-permute-done.5
  64.1 0.3 collective-permute-done.4
  64.4 1.3 %fusion.13 = f32[256,256]{1,0:T(8,128)S(1)} fusion(f32[256,256]{1,0:T(8,128)} %collective-permute-done.5, f32[256,256]{1,0:T(8,128)} %collective-permute-done.4, f32[4,256,256]{2,1,0:T(8,128)} %collective-permute-done.2, f32[4,256,256]{2,1,0:T(8,128)} %collective-permute-done.1, f32[4,256,256]{2,1,0:T(8,128)S(1)} %get-tuple-element.10), kind=kLoop, calls=%fused_computation.30 | loop fusion | flops 262144 | bytes 1572864 | tf_op jit(solution)/shard_map/add | solution.py:168
  65.7 1.1 collective-permute-done.9
  66.8 0.8 collective-permute-done.11
  67.6 1.1 fusion.6
  68.7 0.9 maximum_add_fusion.blend
  69.6 3.4 %shard_map.72.chosen = f32[8,128,1]{2,1,0:T(8,128)} custom-call(f32[256,512]{1,0:T(8,128)} %maximum_add_fusion.blend, f32[8,128,256]{2,1,0:T(8,128)} %broadcast_select_fusion.left, f32[8,128,64]{2,1,0:T(8,128)} %fusion.16.right), custom_call_target="tpu_custom_call" | custom-call | tf_op jit(solution)/shard_map/pallas_call | solution.py:169
  73.0 4.9 %shard_map.73 = f32[512,2,128]{2,1,0:T(2,128)} custom-call(f32[256,512]{1,0:T(8,128)} %maximum_add_fusion.blend, f32[8,128,1]{2,1,0:T(8,128)} %shard_map.72.chosen, f32[8,128,256]{2,1,0:T(8,128)} %broadcast_select_fusion.left, f32[8,128,64]{2,1,0:T(8,128)} %fusion.16.right), custom_call_target="tpu_custom_call" | custom-call | tf_op jit(solution)/shard_map/pallas_call | solution.py:176
  78.0 1.2 %copy.31 = f32[8,128,1]{1,2,0:T(1,128)S(1)} copy(f32[8,128,1]{2,1,0:T(8,128)} %shard_map.72.chosen) | data formatting | bytes 8192 | tf_op jit(solution)/shard_map/pallas_call | solution.py:169
  79.2 28.0 %all-gather = f32[128,128,1]{1,2,0:T(1,128)S(1)} all-gather(f32[8,128,1]{1,2,0:T(1,128)S(1)} %copy.31), channel_id=2, replica_groups=mesh['dp'=16,'mp'=16] {'dp'}, dimensions={0}, use_global_device_ids=true | all-gather | bytes 69632 | tf_op jit(solution)/shard_map/all_gather | solution.py:174
  107.2 4.7 %copy.32.gathered = f32[16,8,128,1]{3,2,1,0:T(8,128)} copy(f32[16,8,128,1]{2,1,0,3:T(8,128)S(1)} %bitcast.47) | data formatting | bytes 131072 | tf_op jit(solution)/shard_map/broadcast_in_dim | solution.py:174
  111.9 6.4 %shard_map.74 = f32[512,2,128]{2,1,0:T(2,128)} custom-call(f32[16,8,128,1]{3,2,1,0:T(8,128)} %copy.32.gathered, f32[8,128,256]{2,1,0:T(8,128)} %broadcast_select_fusion.left, f32[8,128,64]{2,1,0:T(8,128)} %fusion.16.right), custom_call_target="tpu_custom_call" | custom-call | tf_op jit(solution)/shard_map/pallas_call | solution.py:177
  (12 shorter events, 0.1 us)
Async XLA Ops:
  2.1 4.0 %copy-start = (bf16[640,8192]{1,0:T(8,128)(2,1)S(1)}, bf16[640,8192]{1,0:T(8,128)(2,1)}, u32[]{:S(2)}) copy-start(bf16[640,8192]{1,0:T(8,128)(2,1)} %tokens.7) | copy-start | bytes 31457284
  6.1 6.2 %copy-start.1 = (bf16[640,8192]{1,0:T(8,128)(2,1)S(1)}, bf16[640,8192]{1,0:T(8,128)(2,1)}, u32[]{:S(2)}) copy-start(bf16[640,8192]{1,0:T(8,128)(2,1)} %tokens.7) | copy-start | bytes 31457284
  9.6 15.2 %collective-permute-start = (f32[4,256,256]{2,1,0:T(8,128)}, f32[4,256,256]{2,1,0:T(8,128)}, u32[]{:S(2)}, u32[]{:S(2)}) collective-permute-start(f32[4,256,256]{2,1,0:T(8,128)} %get-tuple-element.12), channel_id=1, source_target_pairs={{0,12},{1,13},{2,14},{3,15},{4,0},{5,1},{6,2},{7,3},{8,4},{9,5},{1... | collective-permute-start | bytes 3145736 | tf_op jit(solution)/shard_map/ppermute | solution.py:131
  12.3 19.6 %collective-permute-start.7 = (f32[4,256,256]{2,1,0:T(8,128)}, f32[4,256,256]{2,1,0:T(8,128)}, u32[]{:S(2)}, u32[]{:S(2)}) collective-permute-start(f32[4,256,256]{2,1,0:T(8,128)} %get-tuple-element.17), channel_id=1, source_target_pairs={{0,4},{1,5},{2,6},{3,7},{4,8},{5,9},{6,10},{7,11},{8,12},{9,13},{1... | collective-permute-start | bytes 3145736 | tf_op jit(solution)/shard_map/ppermute | solution.py:131
  12.3 12.4 %copy-start.8 = (s32[8,2,2,32]{3,2,1,0:T(2,128)S(1)}, s32[8,2,2,32]{3,2,1,0:T(2,128)}, u32[]{:S(2)}) copy-start(s32[8,2,2,32]{3,2,1,0:T(2,128)} %param.8) | copy-start | bytes 12292
  12.3 17.8 %copy-start.7 = (f32[64,64,1]{0,1,2:T(8,128)S(1)}, f32[64,64,1]{0,1,2:T(8,128)}, u32[]{:S(2)}) copy-start(f32[64,64,1]{0,1,2:T(8,128)} %constant.140) | copy-start | bytes 49156
  14.6 26.5 %collective-permute-start.2 = (f32[4,256,256]{2,1,0:T(8,128)S(1)}, f32[4,256,256]{2,1,0:T(8,128)}, u32[]{:S(2)}, u32[]{:S(2)}) collective-permute-start(f32[4,256,256]{2,1,0:T(8,128)S(1)} %get-tuple-element.13), channel_id=1, source_target_pairs={{0,4},{1,5},{2,6},{3,7},{4,8},{5,9},{6,10},{7,11},{8,12},{9,13},{1... | collective-permute-start | bytes 3145736 | tf_op jit(solution)/shard_map/ppermute | solution.py:131
  14.7 4.0 %copy-start.2 = (bf16[640,8192]{1,0:T(8,128)(2,1)S(1)}, bf16[640,8192]{1,0:T(8,128)(2,1)}, u32[]{:S(2)}) copy-start(bf16[640,8192]{1,0:T(8,128)(2,1)} %tokens.7) | copy-start | bytes 31457284
  22.0 31.0 %collective-permute-start.6 = (f32[4,256,256]{2,1,0:T(8,128)}, f32[4,256,256]{2,1,0:T(8,128)}, u32[]{:S(2)}, u32[]{:S(2)}) collective-permute-start(f32[4,256,256]{2,1,0:T(8,128)} %get-tuple-element.15), channel_id=1, source_target_pairs={{0,12},{1,13},{2,14},{3,15},{4,0},{5,1},{6,2},{7,3},{8,4},{9,5},{1... | collective-permute-start | bytes 3145736 | tf_op jit(solution)/shard_map/ppermute | solution.py:131
  27.1 20.9 %collective-permute-start.1 = (f32[4,256,256]{2,1,0:T(8,128)}, f32[4,256,256]{2,1,0:T(8,128)}, u32[]{:S(2)}, u32[]{:S(2)}) collective-permute-start(f32[4,256,256]{2,1,0:T(8,128)} %add.255), channel_id=1, source_target_pairs={{0,12},{1,13},{2,14},{3,15},{4,0},{5,1},{6,2},{7,3},{8,4},{9,5},{1... | collective-permute-start | bytes 3145736 | tf_op jit(solution)/shard_map/ppermute | solution.py:131
  31.9 8.0 %copy-start.4 = (f32[8,128,256]{2,1,0:T(8,128)S(1)}, f32[8,128,256]{2,1,0:T(8,128)}, u32[]{:S(2)}) copy-start(f32[8,128,256]{2,1,0:T(8,128)} %copy.28) | copy-start | bytes 3145732
  31.9 18.6 %copy-start.6 = (f32[1,512,2,128]{3,2,1,0:T(2,128)S(1)}, f32[1,512,2,128]{3,2,1,0:T(2,128)}, u32[]{:S(2)}) copy-start(f32[1,512,2,128]{3,2,1,0:T(2,128)} %param.7) | copy-start | bytes 1572868
  33.4 19.6 %collective-permute-start.8 = (f32[4,256,256]{2,1,0:T(8,128)S(1)}, f32[4,256,256]{2,1,0:T(8,128)S(1)}, u32[]{:S(2)}, u32[]{:S(2)}) collective-permute-start(f32[4,256,256]{2,1,0:T(8,128)S(1)} %add.278), channel_id=1, source_target_pairs={{0,4},{1,5},{2,6},{3,7},{4,8},{5,9},{6,10},{7,11},{8,12},{9,13},{1... | collective-permute-start | bytes 3145736 | tf_op jit(solution)/shard_map/ppermute | solution.py:131
  33.5 4.0 %copy-start.3 = (bf16[640,8192]{1,0:T(8,128)(2,1)S(1)}, bf16[640,8192]{1,0:T(8,128)(2,1)}, u32[]{:S(2)}) copy-start(bf16[640,8192]{1,0:T(8,128)(2,1)} %tokens.7) | copy-start | bytes 31457284
  50.0 6.4 %collective-permute-start.3 = (f32[256,256]{1,0:T(8,128)S(1)}, f32[256,256]{1,0:T(8,128)S(1)}, u32[]{:S(2)}, u32[]{:S(2)}) collective-permute-start(f32[256,256]{1,0:T(8,128)S(1)} %get-tuple-element.18), channel_id=1, source_target_pairs={{0,3},{1,0},{2,1},{3,2},{4,7},{5,4},{6,5},{7,6},{8,11},{9,8},{10,9... | collective-permute-start | bytes 786440 | tf_op jit(solution)/shard_map/ppermute | solution.py:131
  50.8 13.3 %collective-permute-start.5 = (f32[256,256]{1,0:T(8,128)}, f32[256,256]{1,0:T(8,128)}, u32[]{:S(2)}, u32[]{:S(2)}) collective-permute-start(f32[256,256]{1,0:T(8,128)} %get-tuple-element.19), channel_id=1, source_target_pairs={{0,1},{1,2},{2,3},{3,0},{4,5},{5,6},{6,7},{7,4},{8,9},{9,10},{10,1... | collective-permute-start | bytes 786440 | tf_op jit(solution)/shard_map/ppermute | solution.py:131
  53.0 5.0 %copy-start.5 = (f32[4,256,256]{2,1,0:T(8,128)}, f32[4,256,256]{2,1,0:T(8,128)S(1)}, u32[]{:S(2)}) copy-start(f32[4,256,256]{2,1,0:T(8,128)S(1)} %collective-permute-done.8) | copy-start | bytes 3145732
  55.3 5.8 %collective-permute-start.10 = (f32[256,256]{1,0:T(8,128)}, f32[256,256]{1,0:T(8,128)}, u32[]{:S(2)}, u32[]{:S(2)}) collective-permute-start(f32[256,256]{1,0:T(8,128)} %get-tuple-element.21), channel_id=1, source_target_pairs={{0,1},{1,2},{2,3},{3,0},{4,5},{5,6},{6,7},{7,4},{8,9},{9,10},{10,1... | collective-permute-start | bytes 786440 | tf_op jit(solution)/shard_map/ppermute | solution.py:131
  57.5 6.9 %collective-permute-start.4 = (f32[256,256]{1,0:T(8,128)S(1)}, f32[256,256]{1,0:T(8,128)}, u32[]{:S(2)}, u32[]{:S(2)}) collective-permute-start(f32[256,256]{1,0:T(8,128)S(1)} %fusion.10), channel_id=1, source_target_pairs={{0,3},{1,0},{2,1},{3,2},{4,7},{5,4},{6,5},{7,6},{8,11},{9,8},{10,9... | collective-permute-start | bytes 786440 | tf_op jit(solution)/shard_map/ppermute | solution.py:131
  59.4 7.4 %collective-permute-start.9 = (f32[256,256]{1,0:T(8,128)}, f32[256,256]{1,0:T(8,128)S(1)}, u32[]{:S(2)}, u32[]{:S(2)}) collective-permute-start(f32[256,256]{1,0:T(8,128)} %get-tuple-element.20), channel_id=1, source_target_pairs={{0,3},{1,0},{2,1},{3,2},{4,7},{5,4},{6,5},{7,6},{8,11},{9,8},{10,9... | collective-permute-start | bytes 786440 | tf_op jit(solution)/shard_map/ppermute | solution.py:131
  62.3 5.3 %collective-permute-start.11 = (f32[256,256]{1,0:T(8,128)S(1)}, f32[256,256]{1,0:T(8,128)S(1)}, u32[]{:S(2)}, u32[]{:S(2)}) collective-permute-start(f32[256,256]{1,0:T(8,128)S(1)} %fusion.2), channel_id=1, source_target_pairs={{0,1},{1,2},{2,3},{3,0},{4,5},{5,6},{6,7},{7,4},{8,9},{9,10},{10,1... | collective-permute-start | bytes 786440 | tf_op jit(solution)/shard_map/ppermute | solution.py:131

commit v2 on v0

v2 whole, which is shorter than its diff:
```python
import functools
import math

import jax
import jax.numpy as jnp
import numpy as np
from jax import lax
from jax.experimental import pallas as pl
from jax.experimental.pallas import tpu as pltpu
from jax.sharding import PartitionSpec as P

SPAN = 64
SIDE = 4
DECAY = 0.9
VMEM = 16 * 1024 * 1024
VMEM_LOCAL = 16 * 1024 * 1024
HIGHEST = lax.Precision.HIGHEST


def dct_basis(n):
    u = np.arange(n)[:, None].astype(np.float64)
    a = np.arange(n)[None, :].astype(np.float64)
    basis = np.cos(math.pi * (2.0 * a + 1.0) * u / (2.0 * n)) * math.sqrt(2.0 / n)
    basis[0] *= math.sqrt(0.5)
    return basis.astype(np.float32)


def swap_pairs(n_dp, primary, flip):
    pairs = []
    n_mp = SIDE * SIDE
    for dp in range(n_dp):
        for x in range(SIDE):
            for y in range(SIDE):
                along_x = (dp % 2 == 0) == primary
                to = (x ^ flip, y) if along_x else (x, y ^ flip)
                pairs.append((dp * n_mp + x * SIDE + y, dp * n_mp + to[0] * SIDE + to[1]))
    return pairs


def block_at(flip_p, flip_s):
    core = lax.axis_index("dp") % 2
    mp = lax.axis_index("mp")
    x, y = mp // SIDE, mp % SIDE
    to_p = jnp.where(core == 0, x, y) ^ flip_p
    to_s = jnp.where(core == 0, y, x) ^ flip_s
    return jnp.where(core == 0, to_p * SIDE + to_s, to_s * SIDE + to_p)


def matmul_kernel(table, grads_t, *refs):
    blocks, outs = refs[: len(refs) // 3], refs[len(refs) // 3 :]
    g = grads_t[...]
    half = outs[0].shape[-1]
    for n, block in enumerate(blocks):
        for h in range(2):
            part = block[:, h * half : (h + 1) * half]
            outs[2 * n + h][0] = jnp.dot(g, part, preferred_element_type=jnp.float32)


def partials(grads_t, tokens, rows, flips):
    cols, toks = grads_t.shape
    half = rows // 2
    groups = len(flips)
    steps = np.array([(flip, k) for flip in flips for k in range(SIDE)], np.int32)
    table = block_at(steps[:, 0], steps[:, 1]).astype(jnp.int32)

    def block(n):
        return pl.BlockSpec((toks, rows), lambda i, t: (0, t[n * SIDE + i]))

    return pl.pallas_call(
        matmul_kernel,
        grid_spec=pltpu.PrefetchScalarGridSpec(
            num_scalar_prefetch=1,
            grid=(SIDE,),
            in_specs=[pl.BlockSpec((cols, toks), lambda i, t: (0, 0))] + [block(n) for n in range(groups)],
            out_specs=[pl.BlockSpec((1, cols, half), lambda i, t: (i, 0, 0))] * (2 * groups),
        ),
        out_shape=[jax.ShapeDtypeStruct((SIDE, cols, half), jnp.float32)] * (2 * groups),
        compiler_params=pltpu.CompilerParams(vmem_limit_bytes=VMEM),
        cost_estimate=pl.CostEstimate(
            flops=2 * groups * SIDE * rows * cols * toks,
            bytes_accessed=groups * SIDE * rows * (2 * toks + 4 * cols),
            transcendentals=0,
        ),
    )(table, grads_t, *[tokens] * groups)


def halves(v):
    high = v.astype(jnp.bfloat16)
    return high, (v - high.astype(jnp.float32)).astype(jnp.bfloat16)


def dot3(a, b):
    dot = functools.partial(jnp.dot, preferred_element_type=jnp.float32)
    return dot(a[0], b[0]) + (dot(a[0], b[1]) + dot(a[1], b[0]))


def prepare_kernel(picked, up, wide, right, left_high, left_low, down_high, down_low):
    spans, kept = picked.shape
    cols = wide.shape[2]
    index = lax.broadcasted_iota(jnp.int32, (SPAN, kept), 0)
    group = kept // (cols // SPAN)

    def same(shape, col_dim):
        col = lax.broadcasted_iota(jnp.int32, shape, col_dim) // SPAN
        return col == lax.broadcasted_iota(jnp.int32, shape, 1 - col_dim) // group

    across, along = same((cols, kept), 0), same((kept, cols), 1)
    first = (((0,), (0,)), ((), ()))
    for i in range(spans):
        place = picked[i : i + 1, :]
        hot_u = (index == place >> 6).astype(jnp.float32).astype(jnp.bfloat16)
        hot_v = (index == place & (SPAN - 1)).astype(jnp.float32).astype(jnp.bfloat16)
        right[i] = jnp.dot(up[0], hot_u, preferred_element_type=jnp.float32) + jnp.dot(
            up[1], hot_u, preferred_element_type=jnp.float32
        )
        for part, (left, down) in enumerate(((left_high, down_high), (left_low, down_low))):
            v = lax.dot_general(wide[part], hot_v, first, preferred_element_type=jnp.float32)
            left[i] = jnp.where(across, v, 0.0).astype(jnp.bfloat16)
            if i < down.shape[0]:
                v = lax.dot_general(hot_v, wide[part], first, preferred_element_type=jnp.float32)
                down[i] = jnp.where(along, v, 0.0).astype(jnp.bfloat16)


def fade_kernel(momentum, faded):
    lanes = momentum.shape[2]
    for m in range(momentum.shape[1]):
        faded[:, m * lanes : (m + 1) * lanes] = DECAY * momentum[:, m, :]


def total_of(parts, faded, step, h):
    half = faded.shape[0] // 2
    total = (parts[h][0][step] + parts[h][1][step] + parts[h][2][step]).T
    return total if step else total + faded[h * half : (h + 1) * half, :]


def kept_kernel(parts, faded, right, left_high, left_low, *chosen):
    rows = faded.shape[0]
    spans = rows // SPAN
    for step in range(SIDE):
        for h in range(2):
            total = total_of(parts, faded, step, h)
            for j in range(spans // 2):
                i = h * (spans // 2) + j
                n = step * spans + i
                values = halves(total[j * SPAN : (j + 1) * SPAN, :])
                w = dot3(values, (left_high[n], left_low[n]))
                chosen[step][i : i + 1, :] = jnp.sum(w * right[n], axis=0, keepdims=True)


def join_kernel(parts, faded, *joined):
    half = faded.shape[0] // 2
    for step in range(SIDE):
        for h in range(2):
            joined[step][h * half : (h + 1) * half, :] = total_of(parts, faded, step, h)


def decode(values, right, down_high, down_low, i):
    return dot3(halves(right[i] * values[i : i + 1, :]), (down_high[i], down_low[i]))


def rest_kernel(joined, chosen, right, down_high, down_low, rest):
    for i in range(down_high.shape[0]):
        rows = slice(i * SPAN, (i + 1) * SPAN)
        rest[rows, :] = joined[rows, :] - decode(chosen, right, down_high, down_low, i)


def last_kernel(pieces, mine, other, right, down_high, down_low, momentum, update):
    mats, lanes = update.shape[1], update.shape[2]
    cols = mats * lanes
    spans = down_high.shape[0]
    summed = mine[...] + other[...]
    decoded = [decode(summed, right, down_high, down_low, i) for i in range(spans)]
    squares = jnp.concatenate([jnp.sum(d * d, axis=0, keepdims=True) for d in decoded], axis=0)
    same = lax.broadcasted_iota(jnp.int32, (cols, cols), 0) // SPAN == (
        lax.broadcasted_iota(jnp.int32, (cols, cols), 1) // SPAN
    )
    power = jnp.dot(
        squares, same.astype(jnp.float32), precision=HIGHEST, preferred_element_type=jnp.float32
    ) / (SPAN * SPAN)
    scale = 1.0 / jnp.sqrt(power + 1e-06)
    for i in range(spans):
        rows = slice(i * SPAN, (i + 1) * SPAN)
        scaled = decoded[i] * scale[i : i + 1, :]
        new = pieces[0][rows, :]
        for piece in pieces[1:]:
            new = new + piece[rows, :]
        for m in range(mats):
            there = slice(m * lanes, (m + 1) * lanes)
            update[rows, m, :] = scaled[:, there]
            momentum[rows, m, :] = new[:, there]


def local(kernel, out_shape, **specs):
    return pl.pallas_call(
        kernel,
        out_shape=out_shape,
        **specs,
        compiler_params=pltpu.CompilerParams(vmem_limit_bytes=VMEM_LOCAL),
    )


def on_device(n_dp, tokens, out_grads, momentum, selected):
    rows, mats, lanes = momentum.shape[1:]
    cols = mats * lanes
    spans = rows // SPAN
    ccols = lanes // SPAN
    kept = selected.shape[-1]
    def send(v, primary, flip):
        return lax.ppermute(v, ("dp", "mp"), swap_pairs(n_dp, primary, flip))

    grads_t = out_grads.reshape(out_grads.shape[0], cols).T
    a_lo, a_hi = partials(grads_t, tokens, rows, (2,))
    ra_lo, ra_hi = send(a_lo, True, 1), send(a_hi, True, 3)
    slots = mats * ccols * kept
    picked, _ = lax.optimization_barrier((selected.reshape(spans, slots), a_lo))
    picked = jnp.concatenate([picked, send(picked, False, 1)])
    near_lo, near_hi, far_lo, far_hi = partials(grads_t, tokens, rows, (1, 3))
    rb_lo = send(near_lo, True, 1)
    rb_hi = send(far_hi, True, 3)
    picked = jnp.concatenate([picked, send(picked, False, 2)])
    own_lo, own_hi = partials(grads_t, tokens, rows, (0,))
    rc_hi = send(near_hi + ra_hi, True, 1)
    rc_lo = send(far_lo + ra_lo, True, 3)
    f32, b16 = jnp.float32, jnp.bfloat16
    basis = dct_basis(SPAN)

    def constant_halves(v):
        high = v.astype(b16)
        return jnp.asarray(np.stack([high, (v - high.astype(np.float32)).astype(b16)]))

    right, left_high, left_low, down_high, down_low = local(
        prepare_kernel,
        [jax.ShapeDtypeStruct((SIDE * spans, SPAN, slots), f32)]
        + [jax.ShapeDtypeStruct((SIDE * spans, cols, slots), b16)] * 2
        + [jax.ShapeDtypeStruct((spans, slots, cols), b16)] * 2,
    )(picked, constant_halves(basis.T), constant_halves(np.tile(basis, (1, cols // SPAN))))
    faded = local(fade_kernel, jax.ShapeDtypeStruct((rows, cols), f32))(momentum[0])
    parts = [[own_lo, rb_lo, rc_lo], [own_hi, rb_hi, rc_hi]]
    chosen = local(kept_kernel, [jax.ShapeDtypeStruct((spans, slots), f32)] * SIDE)(
        parts, faded, right, left_high, left_low
    )
    came = [send(chosen[step], False, step) for step in (2, 1, 3)]
    joined = local(join_kernel, [jax.ShapeDtypeStruct((rows, cols), f32)] * SIDE)(parts, faded)
    pieces = [joined[0]]
    chosen = total = chosen[0] + came[0] + came[1] + came[2]
    for flip, behind in ((1, (2,)), (2, (1, 3)), (4, ()), (12, ())):
        other = lax.ppermute(total, "dp", [(i, i ^ flip) for i in range(n_dp)])
        for step in behind:
            block, _ = lax.optimization_barrier((joined[step], total))
            pieces.append(send(block, False, step))
        mine, total = total, total + other
    out_shape = jax.ShapeDtypeStruct((rows, mats, lanes), f32)
    pieces[0] = local(rest_kernel, jax.ShapeDtypeStruct((rows, cols), f32))(
        joined[0], chosen, right, down_high, down_low
    )
    new_momentum, update = local(last_kernel, [out_shape, out_shape])(
        pieces, mine, other, right, down_high, down_low
    )
    return new_momentum[None], update


def solution(mesh):
    return jax.shard_map(
        functools.partial(on_device, mesh.shape["dp"]),
        mesh=mesh,
        in_specs=(
            P(("dp", "mp"), None),
            P(("dp", "mp"), None, None),
            P("dp", "mp", None, None),
            P("mp", None, None, None),
        ),
        out_specs=(P("dp", "mp", None, None), P("mp", None, None)),
        check_vma=False,
    )
```

time: 234 us -> 82.8 us (0.35)
  waiting for transfers between devices: 153 us -> 21.5 us
  starting transfers between devices: 0.04 us -> 31 us
  matrix products: 19.6 us -> 0 us
  blocking collectives: 17.8 us -> 0 us
  Pallas kernels: 0 us -> 17.5 us
  between operations: 14.2 us -> 0.84 us
  local copies, waits for them, and re-layouts: 20 us -> 9.4 us
  other arithmetic: 7.25 us -> 2.26 us
    psum x1 -> x0, waiting for transfers between devices: 153 us -> none  [on_device(): lax.psum(lax.dot_general(tokens, flat_grads, (((0,), (0,)), ((), ())), pr...]
    ppermute x0 -> x18, starting transfers between devices: none -> 31 us  [the longest x14 19.6 us: send(): return lax.ppermute(v, ('dp', 'mp'), swap_pairs(n_dp, primary, flip))]
    ppermute x0 -> x18, waiting for transfers between devices: none -> 21.5 us  [the longest x14 17 us: send(): return lax.ppermute(v, ('dp', 'mp'), swap_pairs(n_dp, primary, flip))]
    dot_general x7 -> x0, matrix products: 19.6 us -> none  [the longest x1 10.7 us: on_device(): lax.dot_general(tokens, flat_grads, (((0,), (0,)), ((), ())), preferred_e...]
    all_gather x1 -> x0, blocking collectives: 17.8 us -> none  [on_device(): gathered = lax.all_gather(packed, 'dp', axis=0, tiled=True)]
    pallas_call x0 -> x9, Pallas kernels: none -> 17.5 us  [the longest x3 8.61 us: partials(): pl.pallas_call(matmul_kernel, grid_spec=pltpu.PrefetchScalarGridSpec(num_...]
    gather x3 -> x0, local copies, waits for them, and re-layouts: 11.7 us -> none  [on_device(): chosen = jnp.take_along_axis(coeffs, selected, axis=3)]
    reduce_sum x2 -> x0, other arithmetic: 6.72 us -> none  [the longest x1 6.67 us: spread_values(): return jnp.sum(jnp.where(matches, values[..., None], 0.0), axis=-2)]
  transfers between devices with their start and end apart: 1 -> 18, of which waited for: 1 -> 7; matrix products, arithmetic and copies ran while one was open for 0% -> 3% of each run, Pallas kernels for 0% -> 13%
where the time goes in v2:
time: 82.8 us; the launch traced here: 82.5 us
  starting transfers between devices  31 us (37%)
  waiting for transfers between devices  21.5 us (26%)
  Pallas kernels  17.5 us (21%)
  local copies, waits for them, and re-layouts  9.4 us (11%)
  other arithmetic  2.26 us (3%)
  between operations  0.84 us (1%)
    ppermute x14, starting transfers between devices, send(): return lax.ppermute(v, ('dp', 'mp'), swap_pairs(n_dp, primary, flip))  19.6 us
    ppermute x14, waiting for transfers between devices, send(): return lax.ppermute(v, ('dp', 'mp'), swap_pairs(n_dp, primary, flip))  17 us
    ppermute x4, starting transfers between devices, on_device(): other = lax.ppermute(total, 'dp', [(i, i ^ flip) for i in range(n_dp)])  11.4 us
    unnamed x17, local copies, waits for them, and re-layouts  9.32 us
    pallas_call x3, Pallas kernels, partials(): pl.pallas_call(matmul_kernel, grid_spec=pltpu.PrefetchScalarGridSpec(num_...  8.61 us
    ppermute x4, waiting for transfers between devices, on_device(): other = lax.ppermute(total, 'dp', [(i, i ^ flip) for i in range(n_dp)])  4.5 us
    pallas_call x1, Pallas kernels, on_device(): local(kept_kernel, [jax.ShapeDtypeStruct((spans, slots), f32)] * SIDE)  2.3 us
    pallas_call x1, Pallas kernels, on_device(): local(last_kernel, [out_shape, out_shape])  2.04 us
  transfers between devices with their start and end apart: 18, of which 7 were waited for; matrix products, arithmetic and copies ran while one was open for 3% of the time, Pallas kernels for 13%

profile of v2, /device:TPU:8, one launch (start us, length us, event | category | flops | bytes accessed | tf_op | source)
XLA Modules:
  0.0 82.5 jit_solution(18175578107063724940)
XLA Ops:
  0.7 1.3 %copy.14 = bf16[640,2,128]{0,2,1:T(8,128)(2,1)S(1)} copy(bf16[640,2,128]{2,1,0:T(2,128)(2,1)} %param.13) | data formatting | bytes 655360 | tf_op args[1]
  2.0 0.0 copy-start
  2.0 4.0 %copy-done = bf16[640,8192]{1,0:T(8,128)(2,1)S(1)} copy-done((bf16[640,8192]{1,0:T(8,128)(2,1)S(1)}, bf16[640,8192]{1,0:T(8,128)(2,1)}, u32[]{:S(2)}) %copy-start) | copy-done | bytes 10485784
  6.0 0.0 copy-start.6
  6.0 0.0 copy-start.7
  6.0 2.3 %shard_map.133 = (f32[4,256,256]{2,1,0:T(8,128)S(1)}, f32[4,256,256]{2,1,0:T(8,128)S(1)}) custom-call(s32[4]{0:T(128)S(1)} %get-tuple-element.56.table, bf16[256,640]{1,0:T(8,128)(2,1)S(1)} %bitcast.5, bf16[640,8192]{1,0:T(8,128)(2,1)S(1)} %copy-done), custom_call_target="tpu_custom_call" | custom-call | flops 671088640 | bytes 4718592 | tf_op jit(solution)/shard_map/pallas_call | solution.py:69
  8.3 1.6 %collective-permute-start.1 = (f32[4,256,256]{2,1,0:T(8,128)S(1)}, f32[4,256,256]{2,1,0:T(8,128)S(1)}, u32[]{:S(2)}, u32[]{:S(2)}) collective-permute-start(f32[4,256,256]{2,1,0:T(8,128)S(1)} %get-tuple-element.32), channel_id=1, source_target_pairs={{0,4},{1,5},{2,6},{3,7},{4,0},{5,1},{6,2},{7,3},{8,12},{9,13},{10,... | collective-permute-start | bytes 3145736 | tf_op jit(solution)/shard_map/ppermute | solution.py:209
  9.9 2.1 %collective-permute-start.4 = (f32[4,256,256]{2,1,0:T(8,128)S(1)}, f32[4,256,256]{2,1,0:T(8,128)S(1)}, u32[]{:S(2)}, u32[]{:S(2)}) collective-permute-start(f32[4,256,256]{2,1,0:T(8,128)S(1)} %get-tuple-element.36), channel_id=1, source_target_pairs={{0,12},{1,13},{2,14},{3,15},{4,8},{5,9},{6,10},{7,11},{8,4},{9,5},... | collective-permute-start | bytes 3145736 | tf_op jit(solution)/shard_map/ppermute | solution.py:209
  12.0 0.0 copy-done.6
  12.0 0.0 copy-done.7
  12.0 4.1 %shard_map.132 = (f32[4,256,256]{2,1,0:T(8,128)}, f32[4,256,256]{2,1,0:T(8,128)S(1)}, f32[4,256,256]{2,1,0:T(8,128)S(1)}, f32[4,256,256]{2,1,0:T(8,128)}) custom-call(s32[8]{0:T(128)S(1)} %broadcast_select_fusion.table, bf16[256,640]{1,0:T(8,128)(2,1)S(1)} %bitcast.6, bf16[640,8192]{1,0:T(8,128)(2,1)S(1)} %copy-done, bf16[640,8192]{1,0:T(8,128)(2,1)S(1)} %copy-done), custom_call_target="tpu_custom_call" | custom-call | flops 1342177280 | bytes 9437184 | tf_op jit(solution)/shard_map/pallas_call | solution.py:69
  16.1 0.6 collective-permute-start
  16.6 0.6 collective-permute-start.3
  17.3 5.9 %collective-permute-done.1 = f32[4,256,256]{2,1,0:T(8,128)S(1)} collective-permute-done((f32[4,256,256]{2,1,0:T(8,128)S(1)}, f32[4,256,256]{2,1,0:T(8,128)S(1)}, u32[]{:S(2)}, u32[]{:S(2)}) %collective-permute-start.1) | collective-permute-done | bytes 1048608 | tf_op jit(solution)/shard_map/ppermute | solution.py:209
  23.2 1.1 %add.62 = f32[4,256,256]{2,1,0:T(8,128)} add(f32[4,256,256]{2,1,0:T(8,128)S(1)} %get-tuple-element.31, f32[4,256,256]{2,1,0:T(8,128)S(1)} %collective-permute-done.1) | non-fusion elementwise | flops 262144 | bytes 3145728 | tf_op jit(solution)/shard_map/add | solution.py:223
  24.3 0.0 copy-start.5
  24.3 2.8 %collective-permute-start.2 = (f32[4,256,256]{2,1,0:T(8,128)}, f32[4,256,256]{2,1,0:T(8,128)S(1)}, u32[]{:S(2)}, u32[]{:S(2)}) collective-permute-start(f32[4,256,256]{2,1,0:T(8,128)} %add.62), channel_id=1, source_target_pairs={{0,12},{1,13},{2,14},{3,15},{4,8},{5,9},{6,10},{7,11},{8,4},{9,5},... | collective-permute-start | bytes 3145736 | tf_op jit(solution)/shard_map/ppermute | solution.py:209
  27.1 0.0 collective-permute-done.4
  27.1 1.1 %add.63 = f32[4,256,256]{2,1,0:T(8,128)} add(f32[4,256,256]{2,1,0:T(8,128)S(1)} %get-tuple-element.35, f32[4,256,256]{2,1,0:T(8,128)S(1)} %collective-permute-done.4) | non-fusion elementwise | flops 262144 | bytes 3145728 | tf_op jit(solution)/shard_map/add | solution.py:222
  28.2 0.2 collective-permute-start.5
  28.4 0.0 copy-done.5
  28.4 0.1 reshape.11
  28.5 0.5 collective-permute-start.6
  29.0 3.3 %collective-permute-done.6 = s32[8,128]{1,0:T(8,128)S(1)} collective-permute-done((s32[8,128]{1,0:T(8,128)S(1)}, s32[8,128]{1,0:T(8,128)S(1)}, u32[]{:S(2)}, u32[]{:S(2)}) %collective-permute-start.6) | collective-permute-done | bytes 4128 | tf_op jit(solution)/shard_map/ppermute | solution.py:209
  32.2 2.3 %collective-permute-start.7 = (s32[16,128]{1,0:T(8,128)S(1)}, s32[16,128]{1,0:T(8,128)S(1)}, u32[]{:S(2)}, u32[]{:S(2)}) collective-permute-start(s32[16,128]{1,0:T(8,128)S(1)} %pad_add_fusion.1), channel_id=1, source_target_pairs={{0,2},{1,3},{2,0},{3,1},{4,6},{5,7},{6,4},{7,5},{8,10},{9,11},{10,... | collective-permute-start | bytes 24584 | tf_op jit(solution)/shard_map/ppermute | solution.py:209
  34.5 0.0 copy-start.1
  34.5 4.0 %copy-done.1 = bf16[640,8192]{1,0:T(8,128)(2,1)S(1)} copy-done((bf16[640,8192]{1,0:T(8,128)(2,1)S(1)}, bf16[640,8192]{1,0:T(8,128)(2,1)}, u32[]{:S(2)}) %copy-start.1) | copy-done | bytes 10485784
  38.5 0.0 copy-start.2
  38.5 0.0 copy-start.3
  38.5 2.3 %shard_map.131 = (f32[4,256,256]{2,1,0:T(8,128)S(1)}, f32[4,256,256]{2,1,0:T(8,128)S(1)}) custom-call(s32[4]{0:T(128)S(1)} %get-tuple-element.57.table, bf16[256,640]{1,0:T(8,128)(2,1)S(1)} %bitcast.7, bf16[640,8192]{1,0:T(8,128)(2,1)S(1)} %copy-done.1), custom_call_target="tpu_custom_call" | custom-call | flops 671088640 | bytes 4718592 | tf_op jit(solution)/shard_map/pallas_call | solution.py:69
  40.8 0.0 copy-done.2
  40.8 0.5 shard_map.134.faded
  41.3 0.0 collective-permute-done.7
  41.3 0.0 copy-done.3
  41.3 0.0 copy-done.4
  41.3 1.9 %shard_map.136 = (f32[32,64,128]{2,1,0:T(8,128)S(1)}, bf16[32,256,128]{2,1,0:T(8,128)(2,1)S(1)}, bf16[32,256,128]{2,1,0:T(8,128)(2,1)S(1)}, bf16[8,128,256]{2,1,0:T(8,128)(2,1)S(1)}, bf16[8,128,256]{2,1,0:T(8,128)(2,1)S(1)}) custom-call(s32[32,128]{1,0:T(8,128)S(1)} %pad_add_fusion.picked, bf16[2,64,64]{2,1,0:T(8,128)(2,1)S(1)} %copy-done.4, ...), custom_call_target="tpu_custom_call" | custom-call | tf_op jit(solution)/shard_map/pallas_call | solution.py:231
  43.2 0.0 collective-permute-done.parts_0__1_
  43.2 0.0 collective-permute-done.3.parts_1__1_
  43.3 5.2 %collective-permute-done.2.parts_0__2_ = f32[4,256,256]{2,1,0:T(8,128)S(1)} collective-permute-done((f32[4,256,256]{2,1,0:T(8,128)}, f32[4,256,256]{2,1,0:T(8,128)S(1)}, u32[]{:S(2)}, u32[]{:S(2)}) %collective-permute-start.2) | collective-permute-done | bytes 1048608 | tf_op jit(solution)/shard_map/ppermute | solution.py:209
  48.5 0.0 collective-permute-done.5.parts_1__2_
  48.5 2.3 %shard_map.137 = (f32[8,128]{1,0:T(8,128)S(1)}, f32[8,128]{1,0:T(8,128)S(1)}, f32[8,128]{1,0:T(8,128)S(1)}, f32[8,128]{1,0:T(8,128)S(1)}) custom-call(f32[4,256,256]{2,1,0:T(8,128)S(1)} %get-tuple-element.29.parts_0__0_, f32[4,256,256]{2,1,0:T(8,128)S(1)} %collective-permute-done.parts_0__1_, f32[4,256,256]{2,1,0:T(8,128)S(1)} %collective-permute-done.2.parts_0__2_, ...), custom_call_target="tpu_custom_call" | custom-call | tf_op jit(solution)/shard_map/pallas_call | solution.py:239
  50.8 1.7 %collective-permute-start.10 = (f32[8,128]{1,0:T(8,128)S(1)}, f32[8,128]{1,0:T(8,128)S(1)}, u32[]{:S(2)}, u32[]{:S(2)}) collective-permute-start(f32[8,128]{1,0:T(8,128)S(1)} %get-tuple-element.45), channel_id=1, source_target_pairs={{0,3},{1,2},{2,1},{3,0},{4,7},{5,6},{6,5},{7,4},{8,11},{9,10},{10,... | collective-permute-start | bytes 12296 | tf_op jit(solution)/shard_map/ppermute | solution.py:209
  52.4 1.3 %collective-permute-start.8 = (f32[8,128]{1,0:T(8,128)S(1)}, f32[8,128]{1,0:T(8,128)S(1)}, u32[]{:S(2)}, u32[]{:S(2)}) collective-permute-start(f32[8,128]{1,0:T(8,128)S(1)} %get-tuple-element.43), channel_id=1, source_target_pairs={{0,2},{1,3},{2,0},{3,1},{4,6},{5,7},{6,4},{7,5},{8,10},{9,11},{10,... | collective-permute-start | bytes 12296 | tf_op jit(solution)/shard_map/ppermute | solution.py:209
  53.7 1.2 %collective-permute-start.9 = (f32[8,128]{1,0:T(8,128)S(1)}, f32[8,128]{1,0:T(8,128)S(1)}, u32[]{:S(2)}, u32[]{:S(2)}) collective-permute-start(f32[8,128]{1,0:T(8,128)S(1)} %get-tuple-element.44), channel_id=1, source_target_pairs={{0,1},{1,0},{2,3},{3,2},{4,5},{5,4},{6,7},{7,6},{8,9},{9,8},{10,11... | collective-permute-start | bytes 12296 | tf_op jit(solution)/shard_map/ppermute | solution.py:209
  54.9 0.0 collective-permute-done.10
  54.9 2.6 %collective-permute-done.8 = f32[8,128]{1,0:T(8,128)S(1)} collective-permute-done((f32[8,128]{1,0:T(8,128)S(1)}, f32[8,128]{1,0:T(8,128)S(1)}, u32[]{:S(2)}, u32[]{:S(2)}) %collective-permute-start.8) | collective-permute-done | bytes 4128 | tf_op jit(solution)/shard_map/ppermute | solution.py:209
  57.5 0.0 collective-permute-done.9
  57.5 0.3 collective-permute-start.12
  57.8 1.8 %shard_map.135 = (f32[512,256]{1,0:T(8,128)S(1)}, f32[512,256]{1,0:T(8,128)S(1)}, f32[512,256]{1,0:T(8,128)S(1)}, f32[512,256]{1,0:T(8,128)S(1)}) custom-call(f32[4,256,256]{2,1,0:T(8,128)S(1)} %get-tuple-element.29.parts_0__0_, f32[4,256,256]{2,1,0:T(8,128)S(1)} %collective-permute-done.parts_0__1_, f32[4,256,256]{2,1,0:T(8,128)S(1)} %collective-permute-done.2.parts_0__2_, ...), custom_call_target="tpu_custom_call" | custom-call | tf_op jit(solution)/shard_map/pallas_call | solution.py:243
  59.7 1.8 %collective-permute-start.11 = (f32[512,256]{1,0:T(8,128)S(1)}, f32[512,256]{1,0:T(8,128)S(1)}, u32[]{:S(2)}, u32[]{:S(2)}) collective-permute-start(f32[512,256]{1,0:T(8,128)S(1)} %get-tuple-element.49), channel_id=1, source_target_pairs={{0,2},{1,3},{2,0},{3,1},{4,6},{5,7},{6,4},{7,5},{8,10},{9,11},{10,... | collective-permute-start | bytes 1572872 | tf_op jit(solution)/shard_map/ppermute | solution.py:209
  61.5 0.0 collective-permute-done.12
  61.5 1.6 %collective-permute-start.14 = (f32[512,256]{1,0:T(8,128)S(1)}, f32[512,256]{1,0:T(8,128)S(1)}, u32[]{:S(2)}, u32[]{:S(2)}) collective-permute-start(f32[512,256]{1,0:T(8,128)S(1)} %get-tuple-element.53), channel_id=1, source_target_pairs={{0,3},{1,2},{2,1},{3,0},{4,7},{5,6},{6,5},{7,4},{8,11},{9,10},{10,... | collective-permute-start | bytes 1572872 | tf_op jit(solution)/shard_map/ppermute | solution.py:209
  63.1 1.3 %collective-permute-start.13 = (f32[512,256]{1,0:T(8,128)S(1)}, f32[512,256]{1,0:T(8,128)S(1)}, u32[]{:S(2)}, u32[]{:S(2)}) collective-permute-start(f32[512,256]{1,0:T(8,128)S(1)} %get-tuple-element.51), channel_id=1, source_target_pairs={{0,1},{1,0},{2,3},{3,2},{4,5},{5,4},{6,7},{7,6},{8,9},{9,8},{10,11... | collective-permute-start | bytes 1572872 | tf_op jit(solution)/shard_map/ppermute | solution.py:209
  64.4 1.9 %collective-permute-start.15 = (f32[8,128]{1,0:T(8,128)S(1)}, f32[8,128]{1,0:T(8,128)S(1)}, u32[]{:S(2)}, u32[]{:S(2)}) collective-permute-start(f32[8,128]{1,0:T(8,128)S(1)} %add.67), channel_id=1, source_target_pairs={{0,32},{16,48},{32,0},{48,16},{64,96},{80,112},{96,64},{112,80},{1... | collective-permute-start | bytes 12296 | tf_op jit(solution)/shard_map/ppermute | solution.py:247
  66.4 1.7 %collective-permute-done.15 = f32[8,128]{1,0:T(8,128)S(1)} collective-permute-done((f32[8,128]{1,0:T(8,128)S(1)}, f32[8,128]{1,0:T(8,128)S(1)}, u32[]{:S(2)}, u32[]{:S(2)}) %collective-permute-start.15) | collective-permute-done | bytes 4128 | tf_op jit(solution)/shard_map/ppermute | solution.py:247
  68.1 3.3 %collective-permute-start.16 = (f32[8,128]{1,0:T(8,128)S(1)}, f32[8,128]{1,0:T(8,128)S(1)}, u32[]{:S(2)}, u32[]{:S(2)}) collective-permute-start(f32[8,128]{1,0:T(8,128)S(1)} %add.68), channel_id=1, source_target_pairs={{0,64},{16,80},{32,96},{48,112},{64,0},{80,16},{96,32},{112,48},{1... | collective-permute-start | bytes 12296 | tf_op jit(solution)/shard_map/ppermute | solution.py:247
  71.3 1.6 %collective-permute-done.16 = f32[8,128]{1,0:T(8,128)S(1)} collective-permute-done((f32[8,128]{1,0:T(8,128)S(1)}, f32[8,128]{1,0:T(8,128)S(1)}, u32[]{:S(2)}, u32[]{:S(2)}) %collective-permute-start.16) | collective-permute-done | bytes 4128 | tf_op jit(solution)/shard_map/ppermute | solution.py:247
  72.9 6.0 %collective-permute-start.17 = (f32[8,128]{1,0:T(8,128)S(1)}, f32[8,128]{1,0:T(8,128)S(1)}, u32[]{:S(2)}, u32[]{:S(2)}) collective-permute-start(f32[8,128]{1,0:T(8,128)S(1)} %add.69.mine), channel_id=1, source_target_pairs={{0,192},{16,208},{32,224},{48,240},{64,128},{80,144},{96,160},{112... | collective-permute-start | bytes 12296 | tf_op jit(solution)/shard_map/ppermute | solution.py:247
  78.9 0.4 shard_map.138.pieces_0_
  79.2 1.2 %collective-permute-done.17.other = f32[8,128]{1,0:T(8,128)S(1)} collective-permute-done((f32[8,128]{1,0:T(8,128)S(1)}, f32[8,128]{1,0:T(8,128)S(1)}, u32[]{:S(2)}, u32[]{:S(2)}) %collective-permute-start.17) | collective-permute-done | bytes 4128 | tf_op jit(solution)/shard_map/ppermute | solution.py:247
  80.5 0.0 collective-permute-done.11.pieces_1_
  80.5 0.0 collective-permute-done.14.pieces_3_
  80.5 0.0 collective-permute-done.13.pieces_2_
  80.5 2.0 %shard_map.139 = (f32[512,2,128]{2,1,0:T(2,128)}, f32[512,2,128]{2,1,0:T(2,128)}) custom-call(f32[512,256]{1,0:T(8,128)S(1)} %shard_map.138.pieces_0_, f32[512,256]{1,0:T(8,128)S(1)} %collective-permute-done.11.pieces_1_, f32[512,256]{1,0:T(8,128)S(1)} %collective-permute-done.13.pieces_2_, f32[512,256]{1,0:T(8,128)S(1)} %collective-permute-done.14.pieces_3_, ...), custom_call_target="tpu_custom_call" | custom-call | tf_op jit(solution)/shard_map/pallas_call | solution.py:256
  (9 shorter events, 0.0 us)
Async XLA Ops:
  2.0 4.0 %copy-start = (bf16[640,8192]{1,0:T(8,128)(2,1)S(1)}, bf16[640,8192]{1,0:T(8,128)(2,1)}, u32[]{:S(2)}) copy-start(bf16[640,8192]{1,0:T(8,128)(2,1)} %refs_0_.5) | copy-start | bytes 31457284
  6.0 6.0 %copy-start.6 = (s32[8]{0:T(128)S(1)}, s32[8]{0:T(128)}, u32[]{:S(2)}) copy-start(s32[8]{0:T(128)} %constant.71.clone) | copy-start | bytes 100
  6.0 6.0 %copy-start.7 = (s32[8]{0:T(128)S(1)}, s32[8]{0:T(128)}, u32[]{:S(2)}) copy-start(s32[8]{0:T(128)} %constant.72.clone) | copy-start | bytes 100
  8.3 14.9 %collective-permute-start.1 = (f32[4,256,256]{2,1,0:T(8,128)S(1)}, f32[4,256,256]{2,1,0:T(8,128)S(1)}, u32[]{:S(2)}, u32[]{:S(2)}) collective-permute-start(f32[4,256,256]{2,1,0:T(8,128)S(1)} %get-tuple-element.32), channel_id=1, source_target_pairs={{0,4},{1,5},{2,6},{3,7},{4,0},{5,1},{6,2},{7,3},{8,12},{9,13},{10,... | collective-permute-start | bytes 3145736 | tf_op jit(solution)/shard_map/ppermute | solution.py:209
  9.9 17.2 %collective-permute-start.4 = (f32[4,256,256]{2,1,0:T(8,128)S(1)}, f32[4,256,256]{2,1,0:T(8,128)S(1)}, u32[]{:S(2)}, u32[]{:S(2)}) collective-permute-start(f32[4,256,256]{2,1,0:T(8,128)S(1)} %get-tuple-element.36), channel_id=1, source_target_pairs={{0,12},{1,13},{2,14},{3,15},{4,8},{5,9},{6,10},{7,11},{8,4},{9,5},... | collective-permute-start | bytes 3145736 | tf_op jit(solution)/shard_map/ppermute | solution.py:209
  16.1 27.2 %collective-permute-start = (f32[4,256,256]{2,1,0:T(8,128)}, f32[4,256,256]{2,1,0:T(8,128)S(1)}, u32[]{:S(2)}, u32[]{:S(2)}) collective-permute-start(f32[4,256,256]{2,1,0:T(8,128)} %get-tuple-element.30), channel_id=1, source_target_pairs={{0,4},{1,5},{2,6},{3,7},{4,0},{5,1},{6,2},{7,3},{8,12},{9,13},{10,... | collective-permute-start | bytes 3145736 | tf_op jit(solution)/shard_map/ppermute | solution.py:209
  16.6 26.6 %collective-permute-start.3 = (f32[4,256,256]{2,1,0:T(8,128)}, f32[4,256,256]{2,1,0:T(8,128)S(1)}, u32[]{:S(2)}, u32[]{:S(2)}) collective-permute-start(f32[4,256,256]{2,1,0:T(8,128)} %get-tuple-element.34), channel_id=1, source_target_pairs={{0,12},{1,13},{2,14},{3,15},{4,8},{5,9},{6,10},{7,11},{8,4},{9,5},... | collective-permute-start | bytes 3145736 | tf_op jit(solution)/shard_map/ppermute | solution.py:209
  24.3 4.1 %copy-start.5 = (s32[8,2,2,32]{3,2,1,0:T(2,128)S(1)}, s32[8,2,2,32]{3,2,1,0:T(2,128)}, u32[]{:S(2)}) copy-start(s32[8,2,2,32]{3,2,1,0:T(2,128)} %param.15) | copy-start | bytes 12292
  24.3 24.1 %collective-permute-start.2 = (f32[4,256,256]{2,1,0:T(8,128)}, f32[4,256,256]{2,1,0:T(8,128)S(1)}, u32[]{:S(2)}, u32[]{:S(2)}) collective-permute-start(f32[4,256,256]{2,1,0:T(8,128)} %add.62), channel_id=1, source_target_pairs={{0,12},{1,13},{2,14},{3,15},{4,8},{5,9},{6,10},{7,11},{8,4},{9,5},... | collective-permute-start | bytes 3145736 | tf_op jit(solution)/shard_map/ppermute | solution.py:209
  28.2 20.3 %collective-permute-start.5 = (f32[4,256,256]{2,1,0:T(8,128)}, f32[4,256,256]{2,1,0:T(8,128)}, u32[]{:S(2)}, u32[]{:S(2)}) collective-permute-start(f32[4,256,256]{2,1,0:T(8,128)} %add.63), channel_id=1, source_target_pairs={{0,4},{1,5},{2,6},{3,7},{4,0},{5,1},{6,2},{7,3},{8,12},{9,13},{10,... | collective-permute-start | bytes 3145736 | tf_op jit(solution)/shard_map/ppermute | solution.py:209
  28.5 3.7 %collective-permute-start.6 = (s32[8,128]{1,0:T(8,128)S(1)}, s32[8,128]{1,0:T(8,128)S(1)}, u32[]{:S(2)}, u32[]{:S(2)}) collective-permute-start(s32[8,128]{1,0:T(8,128)S(1)} %reshape.11), channel_id=1, source_target_pairs={{0,1},{1,0},{2,3},{3,2},{4,5},{5,4},{6,7},{7,6},{8,9},{9,8},{10,11... | collective-permute-start | bytes 12296 | tf_op jit(solution)/shard_map/ppermute | solution.py:209
  32.2 9.1 %collective-permute-start.7 = (s32[16,128]{1,0:T(8,128)S(1)}, s32[16,128]{1,0:T(8,128)S(1)}, u32[]{:S(2)}, u32[]{:S(2)}) collective-permute-start(s32[16,128]{1,0:T(8,128)S(1)} %pad_add_fusion.1), channel_id=1, source_target_pairs={{0,2},{1,3},{2,0},{3,1},{4,6},{5,7},{6,4},{7,5},{8,10},{9,11},{10,... | collective-permute-start | bytes 24584 | tf_op jit(solution)/shard_map/ppermute | solution.py:209
  34.5 4.0 %copy-start.1 = (bf16[640,8192]{1,0:T(8,128)(2,1)S(1)}, bf16[640,8192]{1,0:T(8,128)(2,1)}, u32[]{:S(2)}) copy-start(bf16[640,8192]{1,0:T(8,128)(2,1)} %refs_0_.5) | copy-start | bytes 31457284
  38.5 2.3 %copy-start.2 = (f32[1,512,2,128]{3,2,1,0:T(2,128)S(1)}, f32[1,512,2,128]{3,2,1,0:T(2,128)}, u32[]{:S(2)}) copy-start(f32[1,512,2,128]{3,2,1,0:T(2,128)} %param.14) | copy-start | bytes 1572868
  38.5 2.8 %copy-start.3 = (bf16[2,64,256]{2,1,0:T(8,128)(2,1)S(1)}, bf16[2,64,256]{2,1,0:T(8,128)(2,1)}, u32[]{:S(2)}) copy-start(bf16[2,64,256]{2,1,0:T(8,128)(2,1)} %constant.75.clone.wide) | copy-start | bytes 196612
  38.5 2.8 %copy-start.4 = (bf16[2,64,64]{2,1,0:T(8,128)(2,1)S(1)}, bf16[2,64,64]{2,1,0:T(8,128)(2,1)}, u32[]{:S(2)}) copy-start(bf16[2,64,64]{2,1,0:T(8,128)(2,1)} %constant.74.clone.up) | copy-start | bytes 49156
  50.8 4.2 %collective-permute-start.10 = (f32[8,128]{1,0:T(8,128)S(1)}, f32[8,128]{1,0:T(8,128)S(1)}, u32[]{:S(2)}, u32[]{:S(2)}) collective-permute-start(f32[8,128]{1,0:T(8,128)S(1)} %get-tuple-element.45), channel_id=1, source_target_pairs={{0,3},{1,2},{2,1},{3,0},{4,7},{5,6},{6,5},{7,4},{8,11},{9,10},{10,... | collective-permute-start | bytes 12296 | tf_op jit(solution)/shard_map/ppermute | solution.py:209
  52.4 5.1 %collective-permute-start.8 = (f32[8,128]{1,0:T(8,128)S(1)}, f32[8,128]{1,0:T(8,128)S(1)}, u32[]{:S(2)}, u32[]{:S(2)}) collective-permute-start(f32[8,128]{1,0:T(8,128)S(1)} %get-tuple-element.43), channel_id=1, source_target_pairs={{0,2},{1,3},{2,0},{3,1},{4,6},{5,7},{6,4},{7,5},{8,10},{9,11},{10,... | collective-permute-start | bytes 12296 | tf_op jit(solution)/shard_map/ppermute | solution.py:209
  53.7 3.8 %collective-permute-start.9 = (f32[8,128]{1,0:T(8,128)S(1)}, f32[8,128]{1,0:T(8,128)S(1)}, u32[]{:S(2)}, u32[]{:S(2)}) collective-permute-start(f32[8,128]{1,0:T(8,128)S(1)} %get-tuple-element.44), channel_id=1, source_target_pairs={{0,1},{1,0},{2,3},{3,2},{4,5},{5,4},{6,7},{7,6},{8,9},{9,8},{10,11... | collective-permute-start | bytes 12296 | tf_op jit(solution)/shard_map/ppermute | solution.py:209
  57.5 3.9 %collective-permute-start.12 = (f32[8,128]{1,0:T(8,128)S(1)}, f32[8,128]{1,0:T(8,128)S(1)}, u32[]{:S(2)}, u32[]{:S(2)}) collective-permute-start(f32[8,128]{1,0:T(8,128)S(1)} %add_add_fusion.chosen), channel_id=1, source_target_pairs={{0,16},{16,0},{32,48},{48,32},{64,80},{80,64},{96,112},{112,96},{1... | collective-permute-start | bytes 12296 | tf_op jit(solution)/shard_map/ppermute | solution.py:247
  59.7 20.8 %collective-permute-start.11 = (f32[512,256]{1,0:T(8,128)S(1)}, f32[512,256]{1,0:T(8,128)S(1)}, u32[]{:S(2)}, u32[]{:S(2)}) collective-permute-start(f32[512,256]{1,0:T(8,128)S(1)} %get-tuple-element.49), channel_id=1, source_target_pairs={{0,2},{1,3},{2,0},{3,1},{4,6},{5,7},{6,4},{7,5},{8,10},{9,11},{10,... | collective-permute-start | bytes 1572872 | tf_op jit(solution)/shard_map/ppermute | solution.py:209
  61.5 19.0 %collective-permute-start.14 = (f32[512,256]{1,0:T(8,128)S(1)}, f32[512,256]{1,0:T(8,128)S(1)}, u32[]{:S(2)}, u32[]{:S(2)}) collective-permute-start(f32[512,256]{1,0:T(8,128)S(1)} %get-tuple-element.53), channel_id=1, source_target_pairs={{0,3},{1,2},{2,1},{3,0},{4,7},{5,6},{6,5},{7,4},{8,11},{9,10},{10,... | collective-permute-start | bytes 1572872 | tf_op jit(solution)/shard_map/ppermute | solution.py:209
  63.1 17.4 %collective-permute-start.13 = (f32[512,256]{1,0:T(8,128)S(1)}, f32[512,256]{1,0:T(8,128)S(1)}, u32[]{:S(2)}, u32[]{:S(2)}) collective-permute-start(f32[512,256]{1,0:T(8,128)S(1)} %get-tuple-element.51), channel_id=1, source_target_pairs={{0,1},{1,0},{2,3},{3,2},{4,5},{5,4},{6,7},{7,6},{8,9},{9,8},{10,11... | collective-permute-start | bytes 1572872 | tf_op jit(solution)/shard_map/ppermute | solution.py:209
  64.4 3.6 %collective-permute-start.15 = (f32[8,128]{1,0:T(8,128)S(1)}, f32[8,128]{1,0:T(8,128)S(1)}, u32[]{:S(2)}, u32[]{:S(2)}) collective-permute-start(f32[8,128]{1,0:T(8,128)S(1)} %add.67), channel_id=1, source_target_pairs={{0,32},{16,48},{32,0},{48,16},{64,96},{80,112},{96,64},{112,80},{1... | collective-permute-start | bytes 12296 | tf_op jit(solution)/shard_map/ppermute | solution.py:247
  68.1 4.9 %collective-permute-start.16 = (f32[8,128]{1,0:T(8,128)S(1)}, f32[8,128]{1,0:T(8,128)S(1)}, u32[]{:S(2)}, u32[]{:S(2)}) collective-permute-start(f32[8,128]{1,0:T(8,128)S(1)} %add.68), channel_id=1, source_target_pairs={{0,64},{16,80},{32,96},{48,112},{64,0},{80,16},{96,32},{112,48},{1... | collective-permute-start | bytes 12296 | tf_op jit(solution)/shard_map/ppermute | solution.py:247
  72.9 7.5 %collective-permute-start.17 = (f32[8,128]{1,0:T(8,128)S(1)}, f32[8,128]{1,0:T(8,128)S(1)}, u32[]{:S(2)}, u32[]{:S(2)}) collective-permute-start(f32[8,128]{1,0:T(8,128)S(1)} %add.69.mine), channel_id=1, source_target_pairs={{0,192},{16,208},{32,224},{48,240},{64,128},{80,144},{96,160},{112... | collective-permute-start | bytes 12296 | tf_op jit(solution)/shard_map/ppermute | solution.py:247

commit v3 on v2

--- a/solution.py
+++ b/solution.py
@@ -11,8 +11,9 @@
 
 SPAN = 64
 SIDE = 4
+ORDER = (1, 2, 3, 0)
 DECAY = 0.9
-VMEM = 16 * 1024 * 1024
+VMEM = 20 * 1024 * 1024
 VMEM_LOCAL = 16 * 1024 * 1024
 HIGHEST = lax.Precision.HIGHEST
 
@@ -46,42 +47,31 @@
     return jnp.where(core == 0, to_p * SIDE + to_s, to_s * SIDE + to_p)
 
 
-def matmul_kernel(table, grads_t, *refs):
-    blocks, outs = refs[: len(refs) // 3], refs[len(refs) // 3 :]
-    g = grads_t[...]
+def matmul_kernel(groups, grads_t, tokens, *outs):
     half = outs[0].shape[-1]
-    for n, block in enumerate(blocks):
-        for h in range(2):
-            part = block[:, h * half : (h + 1) * half]
-            outs[2 * n + h][0] = jnp.dot(g, part, preferred_element_type=jnp.float32)
-
-
-def partials(grads_t, tokens, rows, flips):
+    for n, group in enumerate(groups):
+        for i, flips in enumerate(group):
+            for h in range(2):
+                start = (2 * block_at(*flips) + h) * half
+                part = tokens[:, pl.ds(pl.multiple_of(start, half), half)]
+                outs[2 * n + h][i] = jnp.dot(grads_t[...], part, preferred_element_type=jnp.float32)
+
+
+def partials(grads_t, tokens, rows, groups):
     cols, toks = grads_t.shape
-    half = rows // 2
-    groups = len(flips)
-    steps = np.array([(flip, k) for flip in flips for k in range(SIDE)], np.int32)
-    table = block_at(steps[:, 0], steps[:, 1]).astype(jnp.int32)
-
-    def block(n):
-        return pl.BlockSpec((toks, rows), lambda i, t: (0, t[n * SIDE + i]))
-
+    count = sum(map(len, groups))
     return pl.pallas_call(
-        matmul_kernel,
-        grid_spec=pltpu.PrefetchScalarGridSpec(
-            num_scalar_prefetch=1,
-            grid=(SIDE,),
-            in_specs=[pl.BlockSpec((cols, toks), lambda i, t: (0, 0))] + [block(n) for n in range(groups)],
-            out_specs=[pl.BlockSpec((1, cols, half), lambda i, t: (i, 0, 0))] * (2 * groups),
-        ),
-        out_shape=[jax.ShapeDtypeStruct((SIDE, cols, half), jnp.float32)] * (2 * groups),
+        functools.partial(matmul_kernel, groups),
+        out_shape=[
+            jax.ShapeDtypeStruct((len(group), cols, rows // 2), jnp.float32) for group in groups for _ in range(2)
+        ],
         compiler_params=pltpu.CompilerParams(vmem_limit_bytes=VMEM),
         cost_estimate=pl.CostEstimate(
-            flops=2 * groups * SIDE * rows * cols * toks,
-            bytes_accessed=groups * SIDE * rows * (2 * toks + 4 * cols),
+            flops=2 * count * rows * cols * toks,
+            bytes_accessed=count * rows * (2 * toks + 4 * cols),
             transcendentals=0,
         ),
-    )(table, grads_t, *[tokens] * groups)
+    )(grads_t, tokens)
 
 
 def halves(v):
@@ -127,31 +117,38 @@
         faded[:, m * lanes : (m + 1) * lanes] = DECAY * momentum[:, m, :]
 
 
-def total_of(parts, faded, step, h):
-    half = faded.shape[0] // 2
-    total = (parts[h][0][step] + parts[h][1][step] + parts[h][2][step]).T
-    return total if step else total + faded[h * half : (h + 1) * half, :]
-
-
-def kept_kernel(parts, faded, right, left_high, left_low, *chosen):
+def keep(total, n, i, right, left_high, left_low, chosen):
+    for j in range(total.shape[0] // SPAN):
+        values = halves(total[j * SPAN : (j + 1) * SPAN, :])
+        w = dot3(values, (left_high[n + i + j], left_low[n + i + j]))
+        chosen[i + j : i + j + 1, :] = jnp.sum(w * right[n + i + j], axis=0, keepdims=True)
+
+
+def join_kernel(parts, right, left_high, left_low, joined, chosen):
+    spans = chosen[0].shape[0]
+    for step, out in enumerate(chosen):
+        half = joined[step].shape[0] // 2
+        for h in range(2):
+            total = (parts[h][0][step] + parts[h][1][step] + parts[h][2][step]).T
+            joined[step][h * half : (h + 1) * half, :] = total
+            keep(total, (step + 1) * spans, h * (spans // 2), right, left_high, left_low, out)
+
+
+def late_kernel(low, high, came_low, came_high, out_near, out_far):
+    out_near[0] = low[SIDE]
+    out_near[1] = high[SIDE] + came_high[SIDE - 1]
+    out_far[0] = high[SIDE + 1]
+    out_far[1] = low[SIDE + 1] + came_low[SIDE - 1]
+
+
+def own_kernel(parts, faded, right, left_high, left_low, joined, chosen):
     rows = faded.shape[0]
-    spans = rows // SPAN
-    for step in range(SIDE):
-        for h in range(2):
-            total = total_of(parts, faded, step, h)
-            for j in range(spans // 2):
-                i = h * (spans // 2) + j
-                n = step * spans + i
-                values = halves(total[j * SPAN : (j + 1) * SPAN, :])
-                w = dot3(values, (left_high[n], left_low[n]))
-                chosen[step][i : i + 1, :] = jnp.sum(w * right[n], axis=0, keepdims=True)
-
-
-def join_kernel(parts, faded, *joined):
-    half = faded.shape[0] // 2
-    for step in range(SIDE):
-        for h in range(2):
-            joined[step][h * half : (h + 1) * half, :] = total_of(parts, faded, step, h)
+    half = rows // 2
+    for h in range(2):
+        own, near, far = parts[0][h], parts[1], parts[2]
+        total = (own[SIDE - 1] + near[h] + far[1 - h]).T + faded[h * half : (h + 1) * half, :]
+        joined[h * half : (h + 1) * half, :] = total
+        keep(total, 0, h * (chosen.shape[0] // 2), right, left_high, left_low, chosen)
 
 
 def decode(values, right, down_high, down_low, i):
@@ -209,18 +206,30 @@
         return lax.ppermute(v, ("dp", "mp"), swap_pairs(n_dp, primary, flip))
 
     grads_t = out_grads.reshape(out_grads.shape[0], cols).T
-    a_lo, a_hi = partials(grads_t, tokens, rows, (2,))
+    def blocks(flip, seconds=ORDER):
+        return [(flip, k) for k in seconds]
+
+    a_lo, a_hi = partials(grads_t, tokens, rows, [blocks(2)])
     ra_lo, ra_hi = send(a_lo, True, 1), send(a_hi, True, 3)
-    slots = mats * ccols * kept
-    picked, _ = lax.optimization_barrier((selected.reshape(spans, slots), a_lo))
-    picked = jnp.concatenate([picked, send(picked, False, 1)])
-    near_lo, near_hi, far_lo, far_hi = partials(grads_t, tokens, rows, (1, 3))
+    near_lo, near_hi, far_lo, far_hi, own_lo, own_hi = partials(
+        grads_t,
+        tokens,
+        rows,
+        [
+            blocks(1, ORDER[:-1]),
+            blocks(3, ORDER[:-1]),
+            blocks(0) + [(1, ORDER[-1]), (3, ORDER[-1])],
+        ],
+    )
     rb_lo = send(near_lo, True, 1)
     rb_hi = send(far_hi, True, 3)
+    slots = mats * ccols * kept
+    picked, _ = lax.optimization_barrier((selected.reshape(spans, slots), near_lo))
+    picked = jnp.concatenate([picked, send(picked, False, 1)])
+    near_hi, far_lo, picked = lax.optimization_barrier((near_hi, far_lo, picked))
     picked = jnp.concatenate([picked, send(picked, False, 2)])
-    own_lo, own_hi = partials(grads_t, tokens, rows, (0,))
-    rc_hi = send(near_hi + ra_hi, True, 1)
-    rc_lo = send(far_lo + ra_lo, True, 3)
+    rc_hi = send(near_hi + ra_hi[: SIDE - 1], True, 1)
+    rc_lo = send(far_lo + ra_lo[: SIDE - 1], True, 3)
     f32, b16 = jnp.float32, jnp.bfloat16
     basis = dct_basis(SPAN)
 
@@ -235,23 +244,35 @@
         + [jax.ShapeDtypeStruct((spans, slots, cols), b16)] * 2,
     )(picked, constant_halves(basis.T), constant_halves(np.tile(basis, (1, cols // SPAN))))
     faded = local(fade_kernel, jax.ShapeDtypeStruct((rows, cols), f32))(momentum[0])
+    own_lo, own_hi, right, faded = lax.optimization_barrier((own_lo, own_hi, right, faded))
+    late_shape = jax.ShapeDtypeStruct((2, cols, rows // 2), f32)
+    late_near, late_far = local(late_kernel, [late_shape] * 2)(own_lo, own_hi, ra_lo, ra_hi)
+    rf_near = send(late_near, True, 1)
+    rf_far = send(late_far, True, 3)
     parts = [[own_lo, rb_lo, rc_lo], [own_hi, rb_hi, rc_hi]]
-    chosen = local(kept_kernel, [jax.ShapeDtypeStruct((spans, slots), f32)] * SIDE)(
-        parts, faded, right, left_high, left_low
-    )
-    came = [send(chosen[step], False, step) for step in (2, 1, 3)]
-    joined = local(join_kernel, [jax.ShapeDtypeStruct((rows, cols), f32)] * SIDE)(parts, faded)
-    pieces = [joined[0]]
-    chosen = total = chosen[0] + came[0] + came[1] + came[2]
+    joined, chosen = local(
+        join_kernel,
+        [
+            [jax.ShapeDtypeStruct((rows, cols), f32)] * (SIDE - 1),
+            [jax.ShapeDtypeStruct((spans, slots), f32)] * (SIDE - 1),
+        ],
+    )(parts, right, left_high, left_low)
+    came = [send(chosen[flip - 1], False, flip) for flip in (2, 1, 3)]
+    own, chosen = local(
+        own_kernel,
+        [jax.ShapeDtypeStruct((rows, cols), f32), jax.ShapeDtypeStruct((spans, slots), f32)],
+    )([[own_lo, own_hi], rf_near, rf_far], faded, right, left_high, left_low)
+    chosen = total = chosen + came[0] + came[1] + came[2]
+    pieces = [None]
     for flip, behind in ((1, (2,)), (2, (1, 3)), (4, ()), (12, ())):
         other = lax.ppermute(total, "dp", [(i, i ^ flip) for i in range(n_dp)])
         for step in behind:
-            block, _ = lax.optimization_barrier((joined[step], total))
+            block, _ = lax.optimization_barrier((joined[step - 1], total))
             pieces.append(send(block, False, step))
         mine, total = total, total + other
     out_shape = jax.ShapeDtypeStruct((rows, mats, lanes), f32)
     pieces[0] = local(rest_kernel, jax.ShapeDtypeStruct((rows, cols), f32))(
-        joined[0], chosen, right, down_high, down_low
+        own, chosen, right, down_high, down_low
     )
     new_momentum, update = local(last_kernel, [out_shape, out_shape])(
         pieces, mine, other, right, down_high, down_low

time: 82.8 us -> 74.4 us (0.90)
  Pallas kernels: 17.5 us -> 10.9 us
  starting transfers between devices: 31 us -> 33.7 us
  waiting for transfers between devices: 21.5 us -> 19.3 us
  other arithmetic: 2.26 us -> 0.22 us
    pallas_call x5, Pallas kernels: 12.7 us -> 6.11 us  [the longest x2 4.64 us: partials(): pl.pallas_call(functools.partial(matmul_kernel, groups), out_shape=[jax.S...]
    ppermute x14 -> x16, waiting for transfers between devices: 17 us -> 13.8 us  [send(): return lax.ppermute(v, ('dp', 'mp'), swap_pairs(n_dp, primary, flip))]
    ppermute x14 -> x16, starting transfers between devices: 19.6 us -> 22.5 us  [send(): return lax.ppermute(v, ('dp', 'mp'), swap_pairs(n_dp, primary, flip))]
    add x3, other arithmetic: 2.23 us -> 0.21 us  [the longest x1 0.1 us: on_device(): rc_lo = send(far_lo + ra_lo[:SIDE - 1], True, 3)]
    ppermute x4, waiting for transfers between devices: 4.5 us -> 5.52 us  [on_device(): other = lax.ppermute(total, 'dp', [(i, i ^ flip) for i in range(n_dp)])]
    unnamed x17 -> x13, local copies, waits for them, and re-layouts: 9.32 us -> 9.32 us
  transfers between devices with their start and end apart: 18 -> 20, of which waited for: 7 -> 10; matrix products, arithmetic and copies ran while one was open for 3% -> 0% of each run, Pallas kernels for 13% -> 9%
where the time goes in v3:
time: 74.4 us; the launch traced here: 74.3 us
  starting transfers between devices  33.7 us (45%)
  waiting for transfers between devices  19.3 us (26%)
  Pallas kernels  10.9 us (15%)
  local copies, waits for them, and re-layouts  9.4 us (13%)
  between operations  0.76 us (1%)
    ppermute x16, starting transfers between devices, send(): return lax.ppermute(v, ('dp', 'mp'), swap_pairs(n_dp, primary, flip))  22.5 us
    ppermute x16, waiting for transfers between devices, send(): return lax.ppermute(v, ('dp', 'mp'), swap_pairs(n_dp, primary, flip))  13.8 us
    ppermute x4, starting transfers between devices, on_device(): other = lax.ppermute(total, 'dp', [(i, i ^ flip) for i in range(n_dp)])  11.1 us
    unnamed x13, local copies, waits for them, and re-layouts  9.32 us
    ppermute x4, waiting for transfers between devices, on_device(): other = lax.ppermute(total, 'dp', [(i, i ^ flip) for i in range(n_dp)])  5.52 us
    pallas_call x2, Pallas kernels, partials(): pl.pallas_call(functools.partial(matmul_kernel, groups), out_shape=[jax.S...  4.64 us
    pallas_call x1, Pallas kernels, on_device(): local(last_kernel, [out_shape, out_shape])  2.05 us
    pallas_call x1, Pallas kernels, on_device(): local(prepare_kernel, [jax.ShapeDtypeStruct((SIDE * spans, SPAN, slots),...  1.89 us
  transfers between devices with their start and end apart: 20, of which 10 were waited for; matrix products, arithmetic and copies ran while one was open for 0% of the time, Pallas kernels for 9%

profile of v3, /device:TPU:8, one launch (start us, length us, event | category | flops | bytes accessed | tf_op | source)
XLA Modules:
  0.0 74.3 jit_solution(8465507426237382159)
XLA Ops:
  0.6 1.3 %copy.8 = bf16[640,2,128]{0,2,1:T(8,128)(2,1)S(1)} copy(bf16[640,2,128]{2,1,0:T(2,128)(2,1)} %param.7) | data formatting | bytes 655360 | tf_op args[1]
  2.0 0.0 copy-start
  2.0 4.0 %copy-done = bf16[640,8192]{1,0:T(8,128)(2,1)S(1)} copy-done((bf16[640,8192]{1,0:T(8,128)(2,1)S(1)}, bf16[640,8192]{1,0:T(8,128)(2,1)}, u32[]{:S(2)}) %copy-start) | copy-done | bytes 10485784
  6.0 0.0 copy-start.5
  6.0 2.0 %shard_map.80 = (f32[4,256,256]{2,1,0:T(8,128)}, f32[4,256,256]{2,1,0:T(8,128)S(1)}) custom-call(bf16[256,640]{1,0:T(8,128)(2,1)S(1)} %bitcast.5, bf16[640,8192]{1,0:T(8,128)(2,1)S(1)} %copy-done), custom_call_target="tpu_custom_call" | custom-call | flops 671088640 | bytes 4718592 | tf_op jit(solution)/shard_map/pallas_call | solution.py:63
  8.0 1.5 %collective-permute-start.2 = (f32[4,256,256]{2,1,0:T(8,128)}, f32[4,256,256]{2,1,0:T(8,128)S(1)}, u32[]{:S(2)}, u32[]{:S(2)}) collective-permute-start(f32[4,256,256]{2,1,0:T(8,128)} %get-tuple-element.48), channel_id=1, source_target_pairs={{0,4},{1,5},{2,6},{3,7},{4,0},{5,1},{6,2},{7,3},{8,12},{9,13},{10,... | collective-permute-start | bytes 3145736 | tf_op jit(solution)/shard_map/ppermute | solution.py:206
  9.4 2.1 %collective-permute-start.3 = (f32[4,256,256]{2,1,0:T(8,128)S(1)}, f32[4,256,256]{2,1,0:T(8,128)S(1)}, u32[]{:S(2)}, u32[]{:S(2)}) collective-permute-start(f32[4,256,256]{2,1,0:T(8,128)S(1)} %get-tuple-element.49), channel_id=1, source_target_pairs={{0,12},{1,13},{2,14},{3,15},{4,8},{5,9},{6,10},{7,11},{8,4},{9,5},... | collective-permute-start | bytes 3145736 | tf_op jit(solution)/shard_map/ppermute | solution.py:206
  11.5 0.0 copy-done.5
  11.5 0.1 reshape.11
  11.6 0.0 copy-start.1
  11.6 4.0 %copy-done.1 = bf16[640,8192]{1,0:T(8,128)(2,1)S(1)} copy-done((bf16[640,8192]{1,0:T(8,128)(2,1)S(1)}, bf16[640,8192]{1,0:T(8,128)(2,1)}, u32[]{:S(2)}) %copy-start.1) | copy-done | bytes 10485784
  15.6 2.6 %shard_map.77 = (f32[3,256,256]{2,1,0:T(8,128)S(1)}, f32[3,256,256]{2,1,0:T(8,128)S(1)}, f32[3,256,256]{2,1,0:T(8,128)S(1)}, f32[3,256,256]{2,1,0:T(8,128)S(1)},...) custom-call(bf16[256,640]{1,0:T(8,128)(2,1)S(1)} %bitcast.6, bf16[640,8192]{1,0:T(8,128)(2,1)S(1)} %copy-done.1), custom_call_target="tpu_custom_call" | custom-call | flops 2013265920 | bytes 14155776 | tf_op jit(solution)/shard_map/pallas_call | solution.py:63
  18.3 0.5 collective-permute-start
  18.8 0.6 collective-permute-start.6
  19.4 2.2 %collective-permute-start.8 = (f32[3,256,256]{2,1,0:T(8,128)S(1)}, f32[3,256,256]{2,1,0:T(8,128)S(1)}, u32[]{:S(2)}, u32[]{:S(2)}) collective-permute-start(f32[3,256,256]{2,1,0:T(8,128)S(1)} %get-tuple-element.59), channel_id=1, source_target_pairs={{0,12},{1,13},{2,14},{3,15},{4,8},{5,9},{6,10},{7,11},{8,4},{9,5},... | collective-permute-start | bytes 2359304 | tf_op jit(solution)/shard_map/ppermute | solution.py:206
  21.6 0.5 collective-permute-done
  22.1 0.9 %collective-permute-done.2.came_low = f32[4,256,256]{2,1,0:T(8,128)S(1)} collective-permute-done((f32[4,256,256]{2,1,0:T(8,128)}, f32[4,256,256]{2,1,0:T(8,128)S(1)}, u32[]{:S(2)}, u32[]{:S(2)}) %collective-permute-start.2) | collective-permute-done | bytes 1048608 | tf_op jit(solution)/shard_map/ppermute | solution.py:206
  23.0 0.1 slice_add_fusion.1
  23.1 0.0 copy-start.3
  23.1 0.0 copy-start.4
  23.1 2.8 %collective-permute-start.7 = (f32[3,256,256]{2,1,0:T(8,128)S(1)}, f32[3,256,256]{2,1,0:T(8,128)S(1)}, u32[]{:S(2)}, u32[]{:S(2)}) collective-permute-start(f32[3,256,256]{2,1,0:T(8,128)S(1)} %slice_add_fusion.1), channel_id=1, source_target_pairs={{0,12},{1,13},{2,14},{3,15},{4,8},{5,9},{6,10},{7,11},{8,4},{9,5},... | collective-permute-start | bytes 2359304 | tf_op jit(solution)/shard_map/ppermute | solution.py:206
  26.0 0.0 collective-permute-done.3.came_high
  26.0 0.1 slice_add_fusion
  26.1 0.3 collective-permute-start.9
  26.4 2.3 %collective-permute-start.1 = (s32[16,128]{1,0:T(8,128)S(1)}, s32[16,128]{1,0:T(8,128)S(1)}, u32[]{:S(2)}, u32[]{:S(2)}) collective-permute-start(s32[16,128]{1,0:T(8,128)S(1)} %pad_add_fusion.1), channel_id=1, source_target_pairs={{0,2},{1,3},{2,0},{3,1},{4,6},{5,7},{6,4},{7,5},{8,10},{9,11},{10,... | collective-permute-start | bytes 24584 | tf_op jit(solution)/shard_map/ppermute | solution.py:206
  28.7 0.0 copy-done.2
  28.7 0.5 shard_map.79.faded
  29.2 2.5 %collective-permute-done.1 = s32[16,128]{1,0:T(8,128)S(1)} collective-permute-done((s32[16,128]{1,0:T(8,128)S(1)}, s32[16,128]{1,0:T(8,128)S(1)}, u32[]{:S(2)}, u32[]{:S(2)}) %collective-permute-start.1) | collective-permute-done | bytes 8224 | tf_op jit(solution)/shard_map/ppermute | solution.py:206
  31.7 0.0 copy-done.3
  31.7 0.0 copy-done.4
  31.7 1.9 %shard_map.78 = (f32[32,64,128]{2,1,0:T(8,128)S(1)}, bf16[32,256,128]{2,1,0:T(8,128)(2,1)S(1)}, bf16[32,256,128]{2,1,0:T(8,128)(2,1)S(1)}, bf16[8,128,256]{2,1,0:T(8,128)(2,1)S(1)}, bf16[8,128,256]{2,1,0:T(8,128)(2,1)S(1)}) custom-call(s32[32,128]{1,0:T(8,128)S(1)} %pad_add_fusion.picked, bf16[2,64,64]{2,1,0:T(8,128)(2,1)S(1)} %copy-done.4, ...), custom_call_target="tpu_custom_call" | custom-call | tf_op jit(solution)/shard_map/pallas_call | solution.py:240
  33.6 0.1 shard_map.81
  33.7 1.9 %collective-permute-start.4 = (f32[2,256,256]{2,1,0:T(8,128)S(1)}, f32[2,256,256]{2,1,0:T(8,128)S(1)}, u32[]{:S(2)}, u32[]{:S(2)}) collective-permute-start(f32[2,256,256]{2,1,0:T(8,128)S(1)} %get-tuple-element.50), channel_id=1, source_target_pairs={{0,4},{1,5},{2,6},{3,7},{4,0},{5,1},{6,2},{7,3},{8,12},{9,13},{10,... | collective-permute-start | bytes 1572872 | tf_op jit(solution)/shard_map/ppermute | solution.py:206
  35.6 0.0 collective-permute-done.6.parts_0__1_
  35.6 1.6 %collective-permute-start.5 = (f32[2,256,256]{2,1,0:T(8,128)S(1)}, f32[2,256,256]{2,1,0:T(8,128)S(1)}, u32[]{:S(2)}, u32[]{:S(2)}) collective-permute-start(f32[2,256,256]{2,1,0:T(8,128)S(1)} %get-tuple-element.51), channel_id=1, source_target_pairs={{0,12},{1,13},{2,14},{3,15},{4,8},{5,9},{6,10},{7,11},{8,4},{9,5},... | collective-permute-start | bytes 1572872 | tf_op jit(solution)/shard_map/ppermute | solution.py:206
  37.2 0.0 collective-permute-done.8.parts_1__1_
  37.2 5.2 %collective-permute-done.7.parts_0__2_ = f32[3,256,256]{2,1,0:T(8,128)S(1)} collective-permute-done((f32[3,256,256]{2,1,0:T(8,128)S(1)}, f32[3,256,256]{2,1,0:T(8,128)S(1)}, u32[]{:S(2)}, u32[]{:S(2)}) %collective-permute-start.7) | collective-permute-done | bytes 786464 | tf_op jit(solution)/shard_map/ppermute | solution.py:206
  42.4 0.0 collective-permute-done.9.parts_1__2_
  42.4 0.9 %shard_map.83 = (f32[512,256]{1,0:T(8,128)S(1)}, f32[512,256]{1,0:T(8,128)S(1)}, f32[512,256]{1,0:T(8,128)S(1)}, f32[8,128]{1,0:T(8,128)S(1)}, f32[8,128]{1,0:T(8,128)S(1)}, /*index=5*/f32[8,128]{1,0:T(8,128)S(1)}) custom-call(f32[6,256,256]{2,1,0:T(8,128)S(1)} %get-tuple-element.46.low.parts_0__0_, f32[3,256,256]{2,1,0:T(8,128)S(1)} %collective-permute-done.6.parts_0__1_, ...), custom_call_target="tpu_custom_call" | custom-call | tf_op jit(solution)/shard_map/pallas_call | solution.py:253
  43.3 1.7 %collective-permute-start.12 = (f32[8,128]{1,0:T(8,128)S(1)}, f32[8,128]{1,0:T(8,128)S(1)}, u32[]{:S(2)}, u32[]{:S(2)}) collective-permute-start(f32[8,128]{1,0:T(8,128)S(1)} %get-tuple-element.63), channel_id=1, source_target_pairs={{0,3},{1,2},{2,1},{3,0},{4,7},{5,6},{6,5},{7,4},{8,11},{9,10},{10,... | collective-permute-start | bytes 12296 | tf_op jit(solution)/shard_map/ppermute | solution.py:206
  45.0 1.9 %collective-permute-start.11 = (f32[8,128]{1,0:T(8,128)S(1)}, f32[8,128]{1,0:T(8,128)S(1)}, u32[]{:S(2)}, u32[]{:S(2)}) collective-permute-start(f32[8,128]{1,0:T(8,128)S(1)} %get-tuple-element.62), channel_id=1, source_target_pairs={{0,1},{1,0},{2,3},{3,2},{4,5},{5,4},{6,7},{7,6},{8,9},{9,8},{10,11... | collective-permute-start | bytes 12296 | tf_op jit(solution)/shard_map/ppermute | solution.py:206
  46.9 0.0 collective-permute-start.10
  46.9 0.0 collective-permute-done.4.parts_1_
  46.9 1.2 %collective-permute-done.5.parts_2_ = f32[2,256,256]{2,1,0:T(8,128)S(1)} collective-permute-done((f32[2,256,256]{2,1,0:T(8,128)S(1)}, f32[2,256,256]{2,1,0:T(8,128)S(1)}, u32[]{:S(2)}, u32[]{:S(2)}) %collective-permute-start.5) | collective-permute-done | bytes 524320 | tf_op jit(solution)/shard_map/ppermute | solution.py:206
  48.1 0.5 shard_map.82
  48.6 0.0 collective-permute-done.12
  48.6 0.0 collective-permute-done.11
  48.6 3.4 %collective-permute-done.10 = f32[8,128]{1,0:T(8,128)S(1)} collective-permute-done((f32[8,128]{1,0:T(8,128)S(1)}, f32[8,128]{1,0:T(8,128)S(1)}, u32[]{:S(2)}, u32[]{:S(2)}) %collective-permute-start.10) | collective-permute-done | bytes 4128 | tf_op jit(solution)/shard_map/ppermute | solution.py:206
  52.0 0.0 collective-permute-start.14
  52.0 0.1 collective-permute-start.13
  52.1 1.0 %collective-permute-done.14 = f32[8,128]{1,0:T(8,128)S(1)} collective-permute-done((f32[8,128]{1,0:T(8,128)S(1)}, f32[8,128]{1,0:T(8,128)S(1)}, u32[]{:S(2)}, u32[]{:S(2)}) %collective-permute-start.14) | collective-permute-done | bytes 4128 | tf_op jit(solution)/shard_map/ppermute | solution.py:268
  53.2 0.9 %collective-permute-start.15 = (f32[512,256]{1,0:T(8,128)S(1)}, f32[512,256]{1,0:T(8,128)S(1)}, u32[]{:S(2)}, u32[]{:S(2)}) collective-permute-start(f32[512,256]{1,0:T(8,128)S(1)} %get-tuple-element.69), channel_id=1, source_target_pairs={{0,1},{1,0},{2,3},{3,2},{4,5},{5,4},{6,7},{7,6},{8,9},{9,8},{10,11... | collective-permute-start | bytes 1572872 | tf_op jit(solution)/shard_map/ppermute | solution.py:206
  54.0 2.2 %collective-permute-start.16 = (f32[512,256]{1,0:T(8,128)S(1)}, f32[512,256]{1,0:T(8,128)S(1)}, u32[]{:S(2)}, u32[]{:S(2)}) collective-permute-start(f32[512,256]{1,0:T(8,128)S(1)} %get-tuple-element.71), channel_id=1, source_target_pairs={{0,3},{1,2},{2,1},{3,0},{4,7},{5,6},{6,5},{7,4},{8,11},{9,10},{10,... | collective-permute-start | bytes 1572872 | tf_op jit(solution)/shard_map/ppermute | solution.py:206
  56.2 1.9 %collective-permute-start.17 = (f32[8,128]{1,0:T(8,128)S(1)}, f32[8,128]{1,0:T(8,128)S(1)}, u32[]{:S(2)}, u32[]{:S(2)}) collective-permute-start(f32[8,128]{1,0:T(8,128)S(1)} %add.29), channel_id=1, source_target_pairs={{0,32},{16,48},{32,0},{48,16},{64,96},{80,112},{96,64},{112,80},{1... | collective-permute-start | bytes 12296 | tf_op jit(solution)/shard_map/ppermute | solution.py:268
  58.1 1.7 %collective-permute-done.17 = f32[8,128]{1,0:T(8,128)S(1)} collective-permute-done((f32[8,128]{1,0:T(8,128)S(1)}, f32[8,128]{1,0:T(8,128)S(1)}, u32[]{:S(2)}, u32[]{:S(2)}) %collective-permute-start.17) | collective-permute-done | bytes 4128 | tf_op jit(solution)/shard_map/ppermute | solution.py:268
  59.8 3.3 %collective-permute-start.18 = (f32[8,128]{1,0:T(8,128)S(1)}, f32[8,128]{1,0:T(8,128)S(1)}, u32[]{:S(2)}, u32[]{:S(2)}) collective-permute-start(f32[8,128]{1,0:T(8,128)S(1)} %add.30), channel_id=1, source_target_pairs={{0,64},{16,80},{32,96},{48,112},{64,0},{80,16},{96,32},{112,48},{1... | collective-permute-start | bytes 12296 | tf_op jit(solution)/shard_map/ppermute | solution.py:268
  63.1 1.6 %collective-permute-done.18 = f32[8,128]{1,0:T(8,128)S(1)} collective-permute-done((f32[8,128]{1,0:T(8,128)S(1)}, f32[8,128]{1,0:T(8,128)S(1)}, u32[]{:S(2)}, u32[]{:S(2)}) %collective-permute-start.18) | collective-permute-done | bytes 4128 | tf_op jit(solution)/shard_map/ppermute | solution.py:268
  64.7 6.0 %collective-permute-start.19 = (f32[8,128]{1,0:T(8,128)S(1)}, f32[8,128]{1,0:T(8,128)S(1)}, u32[]{:S(2)}, u32[]{:S(2)}) collective-permute-start(f32[8,128]{1,0:T(8,128)S(1)} %add.31.mine), channel_id=1, source_target_pairs={{0,192},{16,208},{32,224},{48,240},{64,128},{80,144},{96,160},{112... | collective-permute-start | bytes 12296 | tf_op jit(solution)/shard_map/ppermute | solution.py:268
  70.6 0.4 shard_map.84.pieces_0_
  71.0 1.2 %collective-permute-done.19.other = f32[8,128]{1,0:T(8,128)S(1)} collective-permute-done((f32[8,128]{1,0:T(8,128)S(1)}, f32[8,128]{1,0:T(8,128)S(1)}, u32[]{:S(2)}, u32[]{:S(2)}) %collective-permute-start.19) | collective-permute-done | bytes 4128 | tf_op jit(solution)/shard_map/ppermute | solution.py:268
  72.2 0.0 collective-permute-done.13.pieces_1_
  72.2 0.0 collective-permute-done.15.pieces_2_
  72.2 0.0 collective-permute-done.16.pieces_3_
  72.2 2.0 %shard_map.85 = (f32[512,2,128]{2,1,0:T(2,128)}, f32[512,2,128]{2,1,0:T(2,128)}) custom-call(f32[512,256]{1,0:T(8,128)S(1)} %shard_map.84.pieces_0_, f32[512,256]{1,0:T(8,128)S(1)} %collective-permute-done.13.pieces_1_, f32[512,256]{1,0:T(8,128)S(1)} %collective-permute-done.15.pieces_2_, f32[512,256]{1,0:T(8,128)S(1)} %collective-permute-done.16.pieces_3_, ...), custom_call_target="tpu_custom_call" | custom-call | tf_op jit(solution)/shard_map/pallas_call | solution.py:277
  (7 shorter events, 0.0 us)
Async XLA Ops:
  2.0 4.0 %copy-start = (bf16[640,8192]{1,0:T(8,128)(2,1)S(1)}, bf16[640,8192]{1,0:T(8,128)(2,1)}, u32[]{:S(2)}) copy-start(bf16[640,8192]{1,0:T(8,128)(2,1)} %tokens.3) | copy-start | bytes 31457284
  6.0 5.6 %copy-start.5 = (s32[8,2,2,32]{3,2,1,0:T(2,128)S(1)}, s32[8,2,2,32]{3,2,1,0:T(2,128)}, u32[]{:S(2)}) copy-start(s32[8,2,2,32]{3,2,1,0:T(2,128)} %param.9) | copy-start | bytes 12292
  8.0 15.1 %collective-permute-start.2 = (f32[4,256,256]{2,1,0:T(8,128)}, f32[4,256,256]{2,1,0:T(8,128)S(1)}, u32[]{:S(2)}, u32[]{:S(2)}) collective-permute-start(f32[4,256,256]{2,1,0:T(8,128)} %get-tuple-element.48), channel_id=1, source_target_pairs={{0,4},{1,5},{2,6},{3,7},{4,0},{5,1},{6,2},{7,3},{8,12},{9,13},{10,... | collective-permute-start | bytes 3145736 | tf_op jit(solution)/shard_map/ppermute | solution.py:206
  9.4 16.5 %collective-permute-start.3 = (f32[4,256,256]{2,1,0:T(8,128)S(1)}, f32[4,256,256]{2,1,0:T(8,128)S(1)}, u32[]{:S(2)}, u32[]{:S(2)}) collective-permute-start(f32[4,256,256]{2,1,0:T(8,128)S(1)} %get-tuple-element.49), channel_id=1, source_target_pairs={{0,12},{1,13},{2,14},{3,15},{4,8},{5,9},{6,10},{7,11},{8,4},{9,5},... | collective-permute-start | bytes 3145736 | tf_op jit(solution)/shard_map/ppermute | solution.py:206
  11.6 4.0 %copy-start.1 = (bf16[640,8192]{1,0:T(8,128)(2,1)S(1)}, bf16[640,8192]{1,0:T(8,128)(2,1)}, u32[]{:S(2)}) copy-start(bf16[640,8192]{1,0:T(8,128)(2,1)} %tokens.3) | copy-start | bytes 31457284
  18.3 3.8 %collective-permute-start = (s32[8,128]{1,0:T(8,128)S(1)}, s32[8,128]{1,0:T(8,128)S(1)}, u32[]{:S(2)}, u32[]{:S(2)}) collective-permute-start(s32[8,128]{1,0:T(8,128)S(1)} %reshape.11), channel_id=1, source_target_pairs={{0,1},{1,0},{2,3},{3,2},{4,5},{5,4},{6,7},{7,6},{8,9},{9,8},{10,11... | collective-permute-start | bytes 12296 | tf_op jit(solution)/shard_map/ppermute | solution.py:206
  18.8 16.8 %collective-permute-start.6 = (f32[3,256,256]{2,1,0:T(8,128)S(1)}, f32[3,256,256]{2,1,0:T(8,128)S(1)}, u32[]{:S(2)}, u32[]{:S(2)}) collective-permute-start(f32[3,256,256]{2,1,0:T(8,128)S(1)} %get-tuple-element.42), channel_id=1, source_target_pairs={{0,4},{1,5},{2,6},{3,7},{4,0},{5,1},{6,2},{7,3},{8,12},{9,13},{10,... | collective-permute-start | bytes 2359304 | tf_op jit(solution)/shard_map/ppermute | solution.py:206
  19.4 17.8 %collective-permute-start.8 = (f32[3,256,256]{2,1,0:T(8,128)S(1)}, f32[3,256,256]{2,1,0:T(8,128)S(1)}, u32[]{:S(2)}, u32[]{:S(2)}) collective-permute-start(f32[3,256,256]{2,1,0:T(8,128)S(1)} %get-tuple-element.59), channel_id=1, source_target_pairs={{0,12},{1,13},{2,14},{3,15},{4,8},{5,9},{6,10},{7,11},{8,4},{9,5},... | collective-permute-start | bytes 2359304 | tf_op jit(solution)/shard_map/ppermute | solution.py:206
  22.1 6.6 %copy-start.2 = (f32[1,512,2,128]{3,2,1,0:T(2,128)S(1)}, f32[1,512,2,128]{3,2,1,0:T(2,128)}, u32[]{:S(2)}) copy-start(f32[1,512,2,128]{3,2,1,0:T(2,128)} %param.8) | copy-start | bytes 1572868
  23.1 8.6 %copy-start.3 = (bf16[2,64,256]{2,1,0:T(8,128)(2,1)S(1)}, bf16[2,64,256]{2,1,0:T(8,128)(2,1)}, u32[]{:S(2)}) copy-start(bf16[2,64,256]{2,1,0:T(8,128)(2,1)} %constant.5.clone.wide) | copy-start | bytes 196612
  23.1 8.6 %copy-start.4 = (bf16[2,64,64]{2,1,0:T(8,128)(2,1)S(1)}, bf16[2,64,64]{2,1,0:T(8,128)(2,1)}, u32[]{:S(2)}) copy-start(bf16[2,64,64]{2,1,0:T(8,128)(2,1)} %constant.4.clone.up) | copy-start | bytes 49156
  23.1 19.3 %collective-permute-start.7 = (f32[3,256,256]{2,1,0:T(8,128)S(1)}, f32[3,256,256]{2,1,0:T(8,128)S(1)}, u32[]{:S(2)}, u32[]{:S(2)}) collective-permute-start(f32[3,256,256]{2,1,0:T(8,128)S(1)} %slice_add_fusion.1), channel_id=1, source_target_pairs={{0,12},{1,13},{2,14},{3,15},{4,8},{5,9},{6,10},{7,11},{8,4},{9,5},... | collective-permute-start | bytes 2359304 | tf_op jit(solution)/shard_map/ppermute | solution.py:206
  26.1 16.3 %collective-permute-start.9 = (f32[3,256,256]{2,1,0:T(8,128)S(1)}, f32[3,256,256]{2,1,0:T(8,128)S(1)}, u32[]{:S(2)}, u32[]{:S(2)}) collective-permute-start(f32[3,256,256]{2,1,0:T(8,128)S(1)} %slice_add_fusion), channel_id=1, source_target_pairs={{0,4},{1,5},{2,6},{3,7},{4,0},{5,1},{6,2},{7,3},{8,12},{9,13},{10,... | collective-permute-start | bytes 2359304 | tf_op jit(solution)/shard_map/ppermute | solution.py:206
  26.4 5.3 %collective-permute-start.1 = (s32[16,128]{1,0:T(8,128)S(1)}, s32[16,128]{1,0:T(8,128)S(1)}, u32[]{:S(2)}, u32[]{:S(2)}) collective-permute-start(s32[16,128]{1,0:T(8,128)S(1)} %pad_add_fusion.1), channel_id=1, source_target_pairs={{0,2},{1,3},{2,0},{3,1},{4,6},{5,7},{6,4},{7,5},{8,10},{9,11},{10,... | collective-permute-start | bytes 24584 | tf_op jit(solution)/shard_map/ppermute | solution.py:206
  33.7 13.2 %collective-permute-start.4 = (f32[2,256,256]{2,1,0:T(8,128)S(1)}, f32[2,256,256]{2,1,0:T(8,128)S(1)}, u32[]{:S(2)}, u32[]{:S(2)}) collective-permute-start(f32[2,256,256]{2,1,0:T(8,128)S(1)} %get-tuple-element.50), channel_id=1, source_target_pairs={{0,4},{1,5},{2,6},{3,7},{4,0},{5,1},{6,2},{7,3},{8,12},{9,13},{10,... | collective-permute-start | bytes 1572872 | tf_op jit(solution)/shard_map/ppermute | solution.py:206
  35.6 12.5 %collective-permute-start.5 = (f32[2,256,256]{2,1,0:T(8,128)S(1)}, f32[2,256,256]{2,1,0:T(8,128)S(1)}, u32[]{:S(2)}, u32[]{:S(2)}) collective-permute-start(f32[2,256,256]{2,1,0:T(8,128)S(1)} %get-tuple-element.51), channel_id=1, source_target_pairs={{0,12},{1,13},{2,14},{3,15},{4,8},{5,9},{6,10},{7,11},{8,4},{9,5},... | collective-permute-start | bytes 1572872 | tf_op jit(solution)/shard_map/ppermute | solution.py:206
  43.3 5.3 %collective-permute-start.12 = (f32[8,128]{1,0:T(8,128)S(1)}, f32[8,128]{1,0:T(8,128)S(1)}, u32[]{:S(2)}, u32[]{:S(2)}) collective-permute-start(f32[8,128]{1,0:T(8,128)S(1)} %get-tuple-element.63), channel_id=1, source_target_pairs={{0,3},{1,2},{2,1},{3,0},{4,7},{5,6},{6,5},{7,4},{8,11},{9,10},{10,... | collective-permute-start | bytes 12296 | tf_op jit(solution)/shard_map/ppermute | solution.py:206
  45.0 3.6 %collective-permute-start.11 = (f32[8,128]{1,0:T(8,128)S(1)}, f32[8,128]{1,0:T(8,128)S(1)}, u32[]{:S(2)}, u32[]{:S(2)}) collective-permute-start(f32[8,128]{1,0:T(8,128)S(1)} %get-tuple-element.62), channel_id=1, source_target_pairs={{0,1},{1,0},{2,3},{3,2},{4,5},{5,4},{6,7},{7,6},{8,9},{9,8},{10,11... | collective-permute-start | bytes 12296 | tf_op jit(solution)/shard_map/ppermute | solution.py:206
  46.9 5.1 %collective-permute-start.10 = (f32[8,128]{1,0:T(8,128)S(1)}, f32[8,128]{1,0:T(8,128)S(1)}, u32[]{:S(2)}, u32[]{:S(2)}) collective-permute-start(f32[8,128]{1,0:T(8,128)S(1)} %get-tuple-element.61), channel_id=1, source_target_pairs={{0,2},{1,3},{2,0},{3,1},{4,6},{5,7},{6,4},{7,5},{8,10},{9,11},{10,... | collective-permute-start | bytes 12296 | tf_op jit(solution)/shard_map/ppermute | solution.py:206
  52.0 1.2 %collective-permute-start.14 = (f32[8,128]{1,0:T(8,128)S(1)}, f32[8,128]{1,0:T(8,128)S(1)}, u32[]{:S(2)}, u32[]{:S(2)}) collective-permute-start(f32[8,128]{1,0:T(8,128)S(1)} %add_add_fusion.chosen), channel_id=1, source_target_pairs={{0,16},{16,0},{32,48},{48,32},{64,80},{80,64},{96,112},{112,96},{1... | collective-permute-start | bytes 12296 | tf_op jit(solution)/shard_map/ppermute | solution.py:268
  52.0 20.2 %collective-permute-start.13 = (f32[512,256]{1,0:T(8,128)S(1)}, f32[512,256]{1,0:T(8,128)S(1)}, u32[]{:S(2)}, u32[]{:S(2)}) collective-permute-start(f32[512,256]{1,0:T(8,128)S(1)} %get-tuple-element.67), channel_id=1, source_target_pairs={{0,2},{1,3},{2,0},{3,1},{4,6},{5,7},{6,4},{7,5},{8,10},{9,11},{10,... | collective-permute-start | bytes 1572872 | tf_op jit(solution)/shard_map/ppermute | solution.py:206
  53.2 19.0 %collective-permute-start.15 = (f32[512,256]{1,0:T(8,128)S(1)}, f32[512,256]{1,0:T(8,128)S(1)}, u32[]{:S(2)}, u32[]{:S(2)}) collective-permute-start(f32[512,256]{1,0:T(8,128)S(1)} %get-tuple-element.69), channel_id=1, source_target_pairs={{0,1},{1,0},{2,3},{3,2},{4,5},{5,4},{6,7},{7,6},{8,9},{9,8},{10,11... | collective-permute-start | bytes 1572872 | tf_op jit(solution)/shard_map/ppermute | solution.py:206
  54.0 18.2 %collective-permute-start.16 = (f32[512,256]{1,0:T(8,128)S(1)}, f32[512,256]{1,0:T(8,128)S(1)}, u32[]{:S(2)}, u32[]{:S(2)}) collective-permute-start(f32[512,256]{1,0:T(8,128)S(1)} %get-tuple-element.71), channel_id=1, source_target_pairs={{0,3},{1,2},{2,1},{3,0},{4,7},{5,6},{6,5},{7,4},{8,11},{9,10},{10,... | collective-permute-start | bytes 1572872 | tf_op jit(solution)/shard_map/ppermute | solution.py:206
  56.2 3.6 %collective-permute-start.17 = (f32[8,128]{1,0:T(8,128)S(1)}, f32[8,128]{1,0:T(8,128)S(1)}, u32[]{:S(2)}, u32[]{:S(2)}) collective-permute-start(f32[8,128]{1,0:T(8,128)S(1)} %add.29), channel_id=1, source_target_pairs={{0,32},{16,48},{32,0},{48,16},{64,96},{80,112},{96,64},{112,80},{1... | collective-permute-start | bytes 12296 | tf_op jit(solution)/shard_map/ppermute | solution.py:268
  59.8 4.9 %collective-permute-start.18 = (f32[8,128]{1,0:T(8,128)S(1)}, f32[8,128]{1,0:T(8,128)S(1)}, u32[]{:S(2)}, u32[]{:S(2)}) collective-permute-start(f32[8,128]{1,0:T(8,128)S(1)} %add.30), channel_id=1, source_target_pairs={{0,64},{16,80},{32,96},{48,112},{64,0},{80,16},{96,32},{112,48},{1... | collective-permute-start | bytes 12296 | tf_op jit(solution)/shard_map/ppermute | solution.py:268
  64.7 7.5 %collective-permute-start.19 = (f32[8,128]{1,0:T(8,128)S(1)}, f32[8,128]{1,0:T(8,128)S(1)}, u32[]{:S(2)}, u32[]{:S(2)}) collective-permute-start(f32[8,128]{1,0:T(8,128)S(1)} %add.31.mine), channel_id=1, source_target_pairs={{0,192},{16,208},{32,224},{48,240},{64,128},{80,144},{96,160},{112... | collective-permute-start | bytes 12296 | tf_op jit(solution)/shard_map/ppermute | solution.py:268

commit v4 on v3

--- a/solution.py
+++ b/solution.py
@@ -264,7 +264,7 @@
     )([[own_lo, own_hi], rf_near, rf_far], faded, right, left_high, left_low)
     chosen = total = chosen + came[0] + came[1] + came[2]
     pieces = [None]
-    for flip, behind in ((1, (2,)), (2, (1, 3)), (4, ()), (12, ())):
+    for flip, behind in ((1, (2, 1)), (2, ()), (4, (3,)), (12, ())):
         other = lax.ppermute(total, "dp", [(i, i ^ flip) for i in range(n_dp)])
         for step in behind:
             block, _ = lax.optimization_barrier((joined[step - 1], total))

time: 74.4 us -> 73.6 us (0.989)
  waiting for transfers between devices: 19.3 us -> 18.4 us
    ppermute x4, waiting for transfers between devices: 5.52 us -> 3.96 us  [on_device(): other = lax.ppermute(total, 'dp', [(i, i ^ flip) for i in range(n_dp)])]
    ppermute x16, starting transfers between devices: 22.5 us -> 23.5 us  [send(): return lax.ppermute(v, ('dp', 'mp'), swap_pairs(n_dp, primary, flip))]
    ppermute x4, starting transfers between devices: 11.1 us -> 10.2 us  [on_device(): other = lax.ppermute(total, 'dp', [(i, i ^ flip) for i in range(n_dp)])]
where the time goes in v4:
time: 73.6 us; the launch traced here: 73.4 us
  starting transfers between devices  33.7 us (46%)
  waiting for transfers between devices  18.4 us (25%)
  Pallas kernels  10.9 us (15%)
  local copies, waits for them, and re-layouts  9.4 us (13%)
  between operations  0.75 us (1%)
    ppermute x16, starting transfers between devices, send(): return lax.ppermute(v, ('dp', 'mp'), swap_pairs(n_dp, primary, flip))  23.5 us
    ppermute x16, waiting for transfers between devices, send(): return lax.ppermute(v, ('dp', 'mp'), swap_pairs(n_dp, primary, flip))  14.5 us
    ppermute x4, starting transfers between devices, on_device(): other = lax.ppermute(total, 'dp', [(i, i ^ flip) for i in range(n_dp)])  10.2 us
    unnamed x13, local copies, waits for them, and re-layouts  9.32 us
    pallas_call x2, Pallas kernels, partials(): pl.pallas_call(functools.partial(matmul_kernel, groups), out_shape=[jax.S...  4.64 us
    ppermute x4, waiting for transfers between devices, on_device(): other = lax.ppermute(total, 'dp', [(i, i ^ flip) for i in range(n_dp)])  3.96 us
    pallas_call x1, Pallas kernels, on_device(): local(last_kernel, [out_shape, out_shape])  2.04 us
    pallas_call x1, Pallas kernels, on_device(): local(prepare_kernel, [jax.ShapeDtypeStruct((SIDE * spans, SPAN, slots),...  1.89 us
  transfers between devices with their start and end apart: 20, of which 10 were waited for; matrix products, arithmetic and copies ran while one was open for 0% of the time, Pallas kernels for 9%

profile of v4, /device:TPU:8, one launch (start us, length us, event | category | flops | bytes accessed | tf_op | source)
XLA Modules:
  0.0 73.4 jit_solution(2243002341260406815)
XLA Ops:
  0.6 1.3 %copy.8 = bf16[640,2,128]{0,2,1:T(8,128)(2,1)S(1)} copy(bf16[640,2,128]{2,1,0:T(2,128)(2,1)} %param.7) | data formatting | bytes 655360 | tf_op args[1]
  2.0 0.0 copy-start
  2.0 4.0 %copy-done = bf16[640,8192]{1,0:T(8,128)(2,1)S(1)} copy-done((bf16[640,8192]{1,0:T(8,128)(2,1)S(1)}, bf16[640,8192]{1,0:T(8,128)(2,1)}, u32[]{:S(2)}) %copy-start) | copy-done | bytes 10485784
  6.0 0.0 copy-start.5
  6.0 2.0 %shard_map.80 = (f32[4,256,256]{2,1,0:T(8,128)}, f32[4,256,256]{2,1,0:T(8,128)S(1)}) custom-call(bf16[256,640]{1,0:T(8,128)(2,1)S(1)} %bitcast.5, bf16[640,8192]{1,0:T(8,128)(2,1)S(1)} %copy-done), custom_call_target="tpu_custom_call" | custom-call | flops 671088640 | bytes 4718592 | tf_op jit(solution)/shard_map/pallas_call | solution.py:63
  8.0 1.5 %collective-permute-start.2 = (f32[4,256,256]{2,1,0:T(8,128)}, f32[4,256,256]{2,1,0:T(8,128)S(1)}, u32[]{:S(2)}, u32[]{:S(2)}) collective-permute-start(f32[4,256,256]{2,1,0:T(8,128)} %get-tuple-element.48), channel_id=1, source_target_pairs={{0,4},{1,5},{2,6},{3,7},{4,0},{5,1},{6,2},{7,3},{8,12},{9,13},{10,... | collective-permute-start | bytes 3145736 | tf_op jit(solution)/shard_map/ppermute | solution.py:206
  9.4 2.1 %collective-permute-start.3 = (f32[4,256,256]{2,1,0:T(8,128)S(1)}, f32[4,256,256]{2,1,0:T(8,128)S(1)}, u32[]{:S(2)}, u32[]{:S(2)}) collective-permute-start(f32[4,256,256]{2,1,0:T(8,128)S(1)} %get-tuple-element.49), channel_id=1, source_target_pairs={{0,12},{1,13},{2,14},{3,15},{4,8},{5,9},{6,10},{7,11},{8,4},{9,5},... | collective-permute-start | bytes 3145736 | tf_op jit(solution)/shard_map/ppermute | solution.py:206
  11.5 0.0 copy-done.5
  11.5 0.1 reshape.11
  11.6 0.0 copy-start.1
  11.6 4.0 %copy-done.1 = bf16[640,8192]{1,0:T(8,128)(2,1)S(1)} copy-done((bf16[640,8192]{1,0:T(8,128)(2,1)S(1)}, bf16[640,8192]{1,0:T(8,128)(2,1)}, u32[]{:S(2)}) %copy-start.1) | copy-done | bytes 10485784
  15.6 2.6 %shard_map.77 = (f32[3,256,256]{2,1,0:T(8,128)S(1)}, f32[3,256,256]{2,1,0:T(8,128)S(1)}, f32[3,256,256]{2,1,0:T(8,128)S(1)}, f32[3,256,256]{2,1,0:T(8,128)S(1)},...) custom-call(bf16[256,640]{1,0:T(8,128)(2,1)S(1)} %bitcast.6, bf16[640,8192]{1,0:T(8,128)(2,1)S(1)} %copy-done.1), custom_call_target="tpu_custom_call" | custom-call | flops 2013265920 | bytes 14155776 | tf_op jit(solution)/shard_map/pallas_call | solution.py:63
  18.3 0.5 collective-permute-start
  18.8 0.6 collective-permute-start.6
  19.4 2.2 %collective-permute-start.8 = (f32[3,256,256]{2,1,0:T(8,128)S(1)}, f32[3,256,256]{2,1,0:T(8,128)S(1)}, u32[]{:S(2)}, u32[]{:S(2)}) collective-permute-start(f32[3,256,256]{2,1,0:T(8,128)S(1)} %get-tuple-element.59), channel_id=1, source_target_pairs={{0,12},{1,13},{2,14},{3,15},{4,8},{5,9},{6,10},{7,11},{8,4},{9,5},... | collective-permute-start | bytes 2359304 | tf_op jit(solution)/shard_map/ppermute | solution.py:206
  21.6 0.5 collective-permute-done
  22.1 0.9 %collective-permute-done.2.came_low = f32[4,256,256]{2,1,0:T(8,128)S(1)} collective-permute-done((f32[4,256,256]{2,1,0:T(8,128)}, f32[4,256,256]{2,1,0:T(8,128)S(1)}, u32[]{:S(2)}, u32[]{:S(2)}) %collective-permute-start.2) | collective-permute-done | bytes 1048608 | tf_op jit(solution)/shard_map/ppermute | solution.py:206
  23.0 0.1 slice_add_fusion.1
  23.1 0.0 copy-start.3
  23.1 0.0 copy-start.4
  23.1 2.8 %collective-permute-start.7 = (f32[3,256,256]{2,1,0:T(8,128)S(1)}, f32[3,256,256]{2,1,0:T(8,128)S(1)}, u32[]{:S(2)}, u32[]{:S(2)}) collective-permute-start(f32[3,256,256]{2,1,0:T(8,128)S(1)} %slice_add_fusion.1), channel_id=1, source_target_pairs={{0,12},{1,13},{2,14},{3,15},{4,8},{5,9},{6,10},{7,11},{8,4},{9,5},... | collective-permute-start | bytes 2359304 | tf_op jit(solution)/shard_map/ppermute | solution.py:206
  26.0 0.0 collective-permute-done.3.came_high
  26.0 0.1 slice_add_fusion
  26.1 0.3 collective-permute-start.9
  26.4 2.3 %collective-permute-start.1 = (s32[16,128]{1,0:T(8,128)S(1)}, s32[16,128]{1,0:T(8,128)S(1)}, u32[]{:S(2)}, u32[]{:S(2)}) collective-permute-start(s32[16,128]{1,0:T(8,128)S(1)} %pad_add_fusion.1), channel_id=1, source_target_pairs={{0,2},{1,3},{2,0},{3,1},{4,6},{5,7},{6,4},{7,5},{8,10},{9,11},{10,... | collective-permute-start | bytes 24584 | tf_op jit(solution)/shard_map/ppermute | solution.py:206
  28.7 0.0 copy-done.2
  28.7 0.5 shard_map.79.faded
  29.2 2.5 %collective-permute-done.1 = s32[16,128]{1,0:T(8,128)S(1)} collective-permute-done((s32[16,128]{1,0:T(8,128)S(1)}, s32[16,128]{1,0:T(8,128)S(1)}, u32[]{:S(2)}, u32[]{:S(2)}) %collective-permute-start.1) | collective-permute-done | bytes 8224 | tf_op jit(solution)/shard_map/ppermute | solution.py:206
  31.7 0.0 copy-done.3
  31.7 0.0 copy-done.4
  31.7 1.9 %shard_map.78 = (f32[32,64,128]{2,1,0:T(8,128)S(1)}, bf16[32,256,128]{2,1,0:T(8,128)(2,1)S(1)}, bf16[32,256,128]{2,1,0:T(8,128)(2,1)S(1)}, bf16[8,128,256]{2,1,0:T(8,128)(2,1)S(1)}, bf16[8,128,256]{2,1,0:T(8,128)(2,1)S(1)}) custom-call(s32[32,128]{1,0:T(8,128)S(1)} %pad_add_fusion.picked, bf16[2,64,64]{2,1,0:T(8,128)(2,1)S(1)} %copy-done.4, ...), custom_call_target="tpu_custom_call" | custom-call | tf_op jit(solution)/shard_map/pallas_call | solution.py:240
  33.6 0.1 shard_map.81
  33.7 1.9 %collective-permute-start.4 = (f32[2,256,256]{2,1,0:T(8,128)S(1)}, f32[2,256,256]{2,1,0:T(8,128)S(1)}, u32[]{:S(2)}, u32[]{:S(2)}) collective-permute-start(f32[2,256,256]{2,1,0:T(8,128)S(1)} %get-tuple-element.50), channel_id=1, source_target_pairs={{0,4},{1,5},{2,6},{3,7},{4,0},{5,1},{6,2},{7,3},{8,12},{9,13},{10,... | collective-permute-start | bytes 1572872 | tf_op jit(solution)/shard_map/ppermute | solution.py:206
  35.6 0.0 collective-permute-done.6.parts_0__1_
  35.6 1.6 %collective-permute-start.5 = (f32[2,256,256]{2,1,0:T(8,128)S(1)}, f32[2,256,256]{2,1,0:T(8,128)S(1)}, u32[]{:S(2)}, u32[]{:S(2)}) collective-permute-start(f32[2,256,256]{2,1,0:T(8,128)S(1)} %get-tuple-element.51), channel_id=1, source_target_pairs={{0,12},{1,13},{2,14},{3,15},{4,8},{5,9},{6,10},{7,11},{8,4},{9,5},... | collective-permute-start | bytes 1572872 | tf_op jit(solution)/shard_map/ppermute | solution.py:206
  37.2 0.0 collective-permute-done.8.parts_1__1_
  37.2 5.2 %collective-permute-done.7.parts_0__2_ = f32[3,256,256]{2,1,0:T(8,128)S(1)} collective-permute-done((f32[3,256,256]{2,1,0:T(8,128)S(1)}, f32[3,256,256]{2,1,0:T(8,128)S(1)}, u32[]{:S(2)}, u32[]{:S(2)}) %collective-permute-start.7) | collective-permute-done | bytes 786464 | tf_op jit(solution)/shard_map/ppermute | solution.py:206
  42.4 0.0 collective-permute-done.9.parts_1__2_
  42.4 0.9 %shard_map.83 = (f32[512,256]{1,0:T(8,128)S(1)}, f32[512,256]{1,0:T(8,128)S(1)}, f32[512,256]{1,0:T(8,128)S(1)}, f32[8,128]{1,0:T(8,128)S(1)}, f32[8,128]{1,0:T(8,128)S(1)}, /*index=5*/f32[8,128]{1,0:T(8,128)S(1)}) custom-call(f32[6,256,256]{2,1,0:T(8,128)S(1)} %get-tuple-element.46.low.parts_0__0_, f32[3,256,256]{2,1,0:T(8,128)S(1)} %collective-permute-done.6.parts_0__1_, ...), custom_call_target="tpu_custom_call" | custom-call | tf_op jit(solution)/shard_map/pallas_call | solution.py:253
  43.3 1.7 %collective-permute-start.12 = (f32[8,128]{1,0:T(8,128)S(1)}, f32[8,128]{1,0:T(8,128)S(1)}, u32[]{:S(2)}, u32[]{:S(2)}) collective-permute-start(f32[8,128]{1,0:T(8,128)S(1)} %get-tuple-element.63), channel_id=1, source_target_pairs={{0,3},{1,2},{2,1},{3,0},{4,7},{5,6},{6,5},{7,4},{8,11},{9,10},{10,... | collective-permute-start | bytes 12296 | tf_op jit(solution)/shard_map/ppermute | solution.py:206
  45.0 1.9 %collective-permute-start.11 = (f32[8,128]{1,0:T(8,128)S(1)}, f32[8,128]{1,0:T(8,128)S(1)}, u32[]{:S(2)}, u32[]{:S(2)}) collective-permute-start(f32[8,128]{1,0:T(8,128)S(1)} %get-tuple-element.62), channel_id=1, source_target_pairs={{0,1},{1,0},{2,3},{3,2},{4,5},{5,4},{6,7},{7,6},{8,9},{9,8},{10,11... | collective-permute-start | bytes 12296 | tf_op jit(solution)/shard_map/ppermute | solution.py:206
  46.9 0.0 collective-permute-start.10
  46.9 0.0 collective-permute-done.4.parts_1_
  46.9 1.2 %collective-permute-done.5.parts_2_ = f32[2,256,256]{2,1,0:T(8,128)S(1)} collective-permute-done((f32[2,256,256]{2,1,0:T(8,128)S(1)}, f32[2,256,256]{2,1,0:T(8,128)S(1)}, u32[]{:S(2)}, u32[]{:S(2)}) %collective-permute-start.5) | collective-permute-done | bytes 524320 | tf_op jit(solution)/shard_map/ppermute | solution.py:206
  48.1 0.5 shard_map.82
  48.6 0.0 collective-permute-done.12
  48.6 0.0 collective-permute-done.11
  48.6 3.4 %collective-permute-done.10 = f32[8,128]{1,0:T(8,128)S(1)} collective-permute-done((f32[8,128]{1,0:T(8,128)S(1)}, f32[8,128]{1,0:T(8,128)S(1)}, u32[]{:S(2)}, u32[]{:S(2)}) %collective-permute-start.10) | collective-permute-done | bytes 4128 | tf_op jit(solution)/shard_map/ppermute | solution.py:206
  52.0 0.0 collective-permute-start.15
  52.0 1.2 %collective-permute-done.15 = f32[8,128]{1,0:T(8,128)S(1)} collective-permute-done((f32[8,128]{1,0:T(8,128)S(1)}, f32[8,128]{1,0:T(8,128)S(1)}, u32[]{:S(2)}, u32[]{:S(2)}) %collective-permute-start.15) | collective-permute-done | bytes 4128 | tf_op jit(solution)/shard_map/ppermute | solution.py:268
  53.2 1.9 %collective-permute-start.16 = (f32[8,128]{1,0:T(8,128)S(1)}, f32[8,128]{1,0:T(8,128)S(1)}, u32[]{:S(2)}, u32[]{:S(2)}) collective-permute-start(f32[8,128]{1,0:T(8,128)S(1)} %add.29), channel_id=1, source_target_pairs={{0,32},{16,48},{32,0},{48,16},{64,96},{80,112},{96,64},{112,80},{1... | collective-permute-start | bytes 12296 | tf_op jit(solution)/shard_map/ppermute | solution.py:268
  55.1 0.0 collective-permute-start.13
  55.1 1.6 %collective-permute-start.14 = (f32[512,256]{1,0:T(8,128)S(1)}, f32[512,256]{1,0:T(8,128)S(1)}, u32[]{:S(2)}, u32[]{:S(2)}) collective-permute-start(f32[512,256]{1,0:T(8,128)S(1)} %get-tuple-element.69), channel_id=1, source_target_pairs={{0,1},{1,0},{2,3},{3,2},{4,5},{5,4},{6,7},{7,6},{8,9},{9,8},{10,11... | collective-permute-start | bytes 1572872 | tf_op jit(solution)/shard_map/ppermute | solution.py:206
  56.8 0.0 collective-permute-done.16
  56.8 2.4 %collective-permute-start.17 = (f32[512,256]{1,0:T(8,128)S(1)}, f32[512,256]{1,0:T(8,128)S(1)}, u32[]{:S(2)}, u32[]{:S(2)}) collective-permute-start(f32[512,256]{1,0:T(8,128)S(1)} %get-tuple-element.71), channel_id=1, source_target_pairs={{0,3},{1,2},{2,1},{3,0},{4,7},{5,6},{6,5},{7,4},{8,11},{9,10},{10,... | collective-permute-start | bytes 1572872 | tf_op jit(solution)/shard_map/ppermute | solution.py:206
  59.2 3.3 %collective-permute-start.18 = (f32[8,128]{1,0:T(8,128)S(1)}, f32[8,128]{1,0:T(8,128)S(1)}, u32[]{:S(2)}, u32[]{:S(2)}) collective-permute-start(f32[8,128]{1,0:T(8,128)S(1)} %add.30), channel_id=1, source_target_pairs={{0,64},{16,80},{32,96},{48,112},{64,0},{80,16},{96,32},{112,48},{1... | collective-permute-start | bytes 12296 | tf_op jit(solution)/shard_map/ppermute | solution.py:268
  62.4 1.6 %collective-permute-done.18 = f32[8,128]{1,0:T(8,128)S(1)} collective-permute-done((f32[8,128]{1,0:T(8,128)S(1)}, f32[8,128]{1,0:T(8,128)S(1)}, u32[]{:S(2)}, u32[]{:S(2)}) %collective-permute-start.18) | collective-permute-done | bytes 4128 | tf_op jit(solution)/shard_map/ppermute | solution.py:268
  64.0 5.1 %collective-permute-start.19 = (f32[8,128]{1,0:T(8,128)S(1)}, f32[8,128]{1,0:T(8,128)S(1)}, u32[]{:S(2)}, u32[]{:S(2)}) collective-permute-start(f32[8,128]{1,0:T(8,128)S(1)} %add.31.mine), channel_id=1, source_target_pairs={{0,192},{16,208},{32,224},{48,240},{64,128},{80,144},{96,160},{112... | collective-permute-start | bytes 12296 | tf_op jit(solution)/shard_map/ppermute | solution.py:268
  69.1 0.4 shard_map.84.pieces_0_
  69.5 1.2 %collective-permute-done.19.other = f32[8,128]{1,0:T(8,128)S(1)} collective-permute-done((f32[8,128]{1,0:T(8,128)S(1)}, f32[8,128]{1,0:T(8,128)S(1)}, u32[]{:S(2)}, u32[]{:S(2)}) %collective-permute-start.19) | collective-permute-done | bytes 4128 | tf_op jit(solution)/shard_map/ppermute | solution.py:268
  70.7 0.0 collective-permute-done.13.pieces_1_
  70.7 0.0 collective-permute-done.14.pieces_2_
  70.7 0.7 collective-permute-done.17.pieces_3_
  71.4 2.0 %shard_map.85 = (f32[512,2,128]{2,1,0:T(2,128)}, f32[512,2,128]{2,1,0:T(2,128)}) custom-call(f32[512,256]{1,0:T(8,128)S(1)} %shard_map.84.pieces_0_, f32[512,256]{1,0:T(8,128)S(1)} %collective-permute-done.13.pieces_1_, f32[512,256]{1,0:T(8,128)S(1)} %collective-permute-done.14.pieces_2_, f32[512,256]{1,0:T(8,128)S(1)} %collective-permute-done.17.pieces_3_, ...), custom_call_target="tpu_custom_call" | custom-call | tf_op jit(solution)/shard_map/pallas_call | solution.py:277
  (7 shorter events, 0.0 us)
Async XLA Ops:
  2.0 4.0 %copy-start = (bf16[640,8192]{1,0:T(8,128)(2,1)S(1)}, bf16[640,8192]{1,0:T(8,128)(2,1)}, u32[]{:S(2)}) copy-start(bf16[640,8192]{1,0:T(8,128)(2,1)} %tokens.3) | copy-start | bytes 31457284
  6.0 5.6 %copy-start.5 = (s32[8,2,2,32]{3,2,1,0:T(2,128)S(1)}, s32[8,2,2,32]{3,2,1,0:T(2,128)}, u32[]{:S(2)}) copy-start(s32[8,2,2,32]{3,2,1,0:T(2,128)} %param.9) | copy-start | bytes 12292
  8.0 15.1 %collective-permute-start.2 = (f32[4,256,256]{2,1,0:T(8,128)}, f32[4,256,256]{2,1,0:T(8,128)S(1)}, u32[]{:S(2)}, u32[]{:S(2)}) collective-permute-start(f32[4,256,256]{2,1,0:T(8,128)} %get-tuple-element.48), channel_id=1, source_target_pairs={{0,4},{1,5},{2,6},{3,7},{4,0},{5,1},{6,2},{7,3},{8,12},{9,13},{10,... | collective-permute-start | bytes 3145736 | tf_op jit(solution)/shard_map/ppermute | solution.py:206
  9.4 16.5 %collective-permute-start.3 = (f32[4,256,256]{2,1,0:T(8,128)S(1)}, f32[4,256,256]{2,1,0:T(8,128)S(1)}, u32[]{:S(2)}, u32[]{:S(2)}) collective-permute-start(f32[4,256,256]{2,1,0:T(8,128)S(1)} %get-tuple-element.49), channel_id=1, source_target_pairs={{0,12},{1,13},{2,14},{3,15},{4,8},{5,9},{6,10},{7,11},{8,4},{9,5},... | collective-permute-start | bytes 3145736 | tf_op jit(solution)/shard_map/ppermute | solution.py:206
  11.6 4.0 %copy-start.1 = (bf16[640,8192]{1,0:T(8,128)(2,1)S(1)}, bf16[640,8192]{1,0:T(8,128)(2,1)}, u32[]{:S(2)}) copy-start(bf16[640,8192]{1,0:T(8,128)(2,1)} %tokens.3) | copy-start | bytes 31457284
  18.3 3.8 %collective-permute-start = (s32[8,128]{1,0:T(8,128)S(1)}, s32[8,128]{1,0:T(8,128)S(1)}, u32[]{:S(2)}, u32[]{:S(2)}) collective-permute-start(s32[8,128]{1,0:T(8,128)S(1)} %reshape.11), channel_id=1, source_target_pairs={{0,1},{1,0},{2,3},{3,2},{4,5},{5,4},{6,7},{7,6},{8,9},{9,8},{10,11... | collective-permute-start | bytes 12296 | tf_op jit(solution)/shard_map/ppermute | solution.py:206
  18.8 16.8 %collective-permute-start.6 = (f32[3,256,256]{2,1,0:T(8,128)S(1)}, f32[3,256,256]{2,1,0:T(8,128)S(1)}, u32[]{:S(2)}, u32[]{:S(2)}) collective-permute-start(f32[3,256,256]{2,1,0:T(8,128)S(1)} %get-tuple-element.42), channel_id=1, source_target_pairs={{0,4},{1,5},{2,6},{3,7},{4,0},{5,1},{6,2},{7,3},{8,12},{9,13},{10,... | collective-permute-start | bytes 2359304 | tf_op jit(solution)/shard_map/ppermute | solution.py:206
  19.4 17.8 %collective-permute-start.8 = (f32[3,256,256]{2,1,0:T(8,128)S(1)}, f32[3,256,256]{2,1,0:T(8,128)S(1)}, u32[]{:S(2)}, u32[]{:S(2)}) collective-permute-start(f32[3,256,256]{2,1,0:T(8,128)S(1)} %get-tuple-element.59), channel_id=1, source_target_pairs={{0,12},{1,13},{2,14},{3,15},{4,8},{5,9},{6,10},{7,11},{8,4},{9,5},... | collective-permute-start | bytes 2359304 | tf_op jit(solution)/shard_map/ppermute | solution.py:206
  22.1 6.6 %copy-start.2 = (f32[1,512,2,128]{3,2,1,0:T(2,128)S(1)}, f32[1,512,2,128]{3,2,1,0:T(2,128)}, u32[]{:S(2)}) copy-start(f32[1,512,2,128]{3,2,1,0:T(2,128)} %param.8) | copy-start | bytes 1572868
  23.1 8.6 %copy-start.3 = (bf16[2,64,256]{2,1,0:T(8,128)(2,1)S(1)}, bf16[2,64,256]{2,1,0:T(8,128)(2,1)}, u32[]{:S(2)}) copy-start(bf16[2,64,256]{2,1,0:T(8,128)(2,1)} %constant.5.clone.wide) | copy-start | bytes 196612
  23.1 8.6 %copy-start.4 = (bf16[2,64,64]{2,1,0:T(8,128)(2,1)S(1)}, bf16[2,64,64]{2,1,0:T(8,128)(2,1)}, u32[]{:S(2)}) copy-start(bf16[2,64,64]{2,1,0:T(8,128)(2,1)} %constant.4.clone.up) | copy-start | bytes 49156
  23.1 19.3 %collective-permute-start.7 = (f32[3,256,256]{2,1,0:T(8,128)S(1)}, f32[3,256,256]{2,1,0:T(8,128)S(1)}, u32[]{:S(2)}, u32[]{:S(2)}) collective-permute-start(f32[3,256,256]{2,1,0:T(8,128)S(1)} %slice_add_fusion.1), channel_id=1, source_target_pairs={{0,12},{1,13},{2,14},{3,15},{4,8},{5,9},{6,10},{7,11},{8,4},{9,5},... | collective-permute-start | bytes 2359304 | tf_op jit(solution)/shard_map/ppermute | solution.py:206
  26.1 16.3 %collective-permute-start.9 = (f32[3,256,256]{2,1,0:T(8,128)S(1)}, f32[3,256,256]{2,1,0:T(8,128)S(1)}, u32[]{:S(2)}, u32[]{:S(2)}) collective-permute-start(f32[3,256,256]{2,1,0:T(8,128)S(1)} %slice_add_fusion), channel_id=1, source_target_pairs={{0,4},{1,5},{2,6},{3,7},{4,0},{5,1},{6,2},{7,3},{8,12},{9,13},{10,... | collective-permute-start | bytes 2359304 | tf_op jit(solution)/shard_map/ppermute | solution.py:206
  26.4 5.3 %collective-permute-start.1 = (s32[16,128]{1,0:T(8,128)S(1)}, s32[16,128]{1,0:T(8,128)S(1)}, u32[]{:S(2)}, u32[]{:S(2)}) collective-permute-start(s32[16,128]{1,0:T(8,128)S(1)} %pad_add_fusion.1), channel_id=1, source_target_pairs={{0,2},{1,3},{2,0},{3,1},{4,6},{5,7},{6,4},{7,5},{8,10},{9,11},{10,... | collective-permute-start | bytes 24584 | tf_op jit(solution)/shard_map/ppermute | solution.py:206
  33.7 13.2 %collective-permute-start.4 = (f32[2,256,256]{2,1,0:T(8,128)S(1)}, f32[2,256,256]{2,1,0:T(8,128)S(1)}, u32[]{:S(2)}, u32[]{:S(2)}) collective-permute-start(f32[2,256,256]{2,1,0:T(8,128)S(1)} %get-tuple-element.50), channel_id=1, source_target_pairs={{0,4},{1,5},{2,6},{3,7},{4,0},{5,1},{6,2},{7,3},{8,12},{9,13},{10,... | collective-permute-start | bytes 1572872 | tf_op jit(solution)/shard_map/ppermute | solution.py:206
  35.6 12.5 %collective-permute-start.5 = (f32[2,256,256]{2,1,0:T(8,128)S(1)}, f32[2,256,256]{2,1,0:T(8,128)S(1)}, u32[]{:S(2)}, u32[]{:S(2)}) collective-permute-start(f32[2,256,256]{2,1,0:T(8,128)S(1)} %get-tuple-element.51), channel_id=1, source_target_pairs={{0,12},{1,13},{2,14},{3,15},{4,8},{5,9},{6,10},{7,11},{8,4},{9,5},... | collective-permute-start | bytes 1572872 | tf_op jit(solution)/shard_map/ppermute | solution.py:206
  43.3 5.3 %collective-permute-start.12 = (f32[8,128]{1,0:T(8,128)S(1)}, f32[8,128]{1,0:T(8,128)S(1)}, u32[]{:S(2)}, u32[]{:S(2)}) collective-permute-start(f32[8,128]{1,0:T(8,128)S(1)} %get-tuple-element.63), channel_id=1, source_target_pairs={{0,3},{1,2},{2,1},{3,0},{4,7},{5,6},{6,5},{7,4},{8,11},{9,10},{10,... | collective-permute-start | bytes 12296 | tf_op jit(solution)/shard_map/ppermute | solution.py:206
  45.0 3.6 %collective-permute-start.11 = (f32[8,128]{1,0:T(8,128)S(1)}, f32[8,128]{1,0:T(8,128)S(1)}, u32[]{:S(2)}, u32[]{:S(2)}) collective-permute-start(f32[8,128]{1,0:T(8,128)S(1)} %get-tuple-element.62), channel_id=1, source_target_pairs={{0,1},{1,0},{2,3},{3,2},{4,5},{5,4},{6,7},{7,6},{8,9},{9,8},{10,11... | collective-permute-start | bytes 12296 | tf_op jit(solution)/shard_map/ppermute | solution.py:206
  46.9 5.1 %collective-permute-start.10 = (f32[8,128]{1,0:T(8,128)S(1)}, f32[8,128]{1,0:T(8,128)S(1)}, u32[]{:S(2)}, u32[]{:S(2)}) collective-permute-start(f32[8,128]{1,0:T(8,128)S(1)} %get-tuple-element.61), channel_id=1, source_target_pairs={{0,2},{1,3},{2,0},{3,1},{4,6},{5,7},{6,4},{7,5},{8,10},{9,11},{10,... | collective-permute-start | bytes 12296 | tf_op jit(solution)/shard_map/ppermute | solution.py:206
  52.0 1.2 %collective-permute-start.15 = (f32[8,128]{1,0:T(8,128)S(1)}, f32[8,128]{1,0:T(8,128)S(1)}, u32[]{:S(2)}, u32[]{:S(2)}) collective-permute-start(f32[8,128]{1,0:T(8,128)S(1)} %add_add_fusion.chosen), channel_id=1, source_target_pairs={{0,16},{16,0},{32,48},{48,32},{64,80},{80,64},{96,112},{112,96},{1... | collective-permute-start | bytes 12296 | tf_op jit(solution)/shard_map/ppermute | solution.py:268
  53.2 3.6 %collective-permute-start.16 = (f32[8,128]{1,0:T(8,128)S(1)}, f32[8,128]{1,0:T(8,128)S(1)}, u32[]{:S(2)}, u32[]{:S(2)}) collective-permute-start(f32[8,128]{1,0:T(8,128)S(1)} %add.29), channel_id=1, source_target_pairs={{0,32},{16,48},{32,0},{48,16},{64,96},{80,112},{96,64},{112,80},{1... | collective-permute-start | bytes 12296 | tf_op jit(solution)/shard_map/ppermute | solution.py:268
  55.1 15.6 %collective-permute-start.13 = (f32[512,256]{1,0:T(8,128)S(1)}, f32[512,256]{1,0:T(8,128)S(1)}, u32[]{:S(2)}, u32[]{:S(2)}) collective-permute-start(f32[512,256]{1,0:T(8,128)S(1)} %get-tuple-element.67), channel_id=1, source_target_pairs={{0,2},{1,3},{2,0},{3,1},{4,6},{5,7},{6,4},{7,5},{8,10},{9,11},{10,... | collective-permute-start | bytes 1572872 | tf_op jit(solution)/shard_map/ppermute | solution.py:206
  55.1 15.6 %collective-permute-start.14 = (f32[512,256]{1,0:T(8,128)S(1)}, f32[512,256]{1,0:T(8,128)S(1)}, u32[]{:S(2)}, u32[]{:S(2)}) collective-permute-start(f32[512,256]{1,0:T(8,128)S(1)} %get-tuple-element.69), channel_id=1, source_target_pairs={{0,1},{1,0},{2,3},{3,2},{4,5},{5,4},{6,7},{7,6},{8,9},{9,8},{10,11... | collective-permute-start | bytes 1572872 | tf_op jit(solution)/shard_map/ppermute | solution.py:206
  56.8 14.6 %collective-permute-start.17 = (f32[512,256]{1,0:T(8,128)S(1)}, f32[512,256]{1,0:T(8,128)S(1)}, u32[]{:S(2)}, u32[]{:S(2)}) collective-permute-start(f32[512,256]{1,0:T(8,128)S(1)} %get-tuple-element.71), channel_id=1, source_target_pairs={{0,3},{1,2},{2,1},{3,0},{4,7},{5,6},{6,5},{7,4},{8,11},{9,10},{10,... | collective-permute-start | bytes 1572872 | tf_op jit(solution)/shard_map/ppermute | solution.py:206
  59.2 4.9 %collective-permute-start.18 = (f32[8,128]{1,0:T(8,128)S(1)}, f32[8,128]{1,0:T(8,128)S(1)}, u32[]{:S(2)}, u32[]{:S(2)}) collective-permute-start(f32[8,128]{1,0:T(8,128)S(1)} %add.30), channel_id=1, source_target_pairs={{0,64},{16,80},{32,96},{48,112},{64,0},{80,16},{96,32},{112,48},{1... | collective-permute-start | bytes 12296 | tf_op jit(solution)/shard_map/ppermute | solution.py:268
  64.0 6.6 %collective-permute-start.19 = (f32[8,128]{1,0:T(8,128)S(1)}, f32[8,128]{1,0:T(8,128)S(1)}, u32[]{:S(2)}, u32[]{:S(2)}) collective-permute-start(f32[8,128]{1,0:T(8,128)S(1)} %add.31.mine), channel_id=1, source_target_pairs={{0,192},{16,208},{32,224},{48,240},{64,128},{80,144},{96,160},{112... | collective-permute-start | bytes 12296 | tf_op jit(solution)/shard_map/ppermute | solution.py:268
